TPU v7x, 32 devices: a whole 2x2x4 slice. The times are simulated.
32 devices in a mesh: leaf: 8 (over y, x, core), sub: 4 (over z).
Axes of the slice: x: 2, y: 2, z: 4, core: 2. Of those that a mesh axis runs over, the one named last changes fastest.
Arguments:
- densities: bfloat16 [16, 131072], P(None, ('leaf', 'sub')), may hold values from -6 to 6
- basis: bfloat16 [512, 64, 256], P(('leaf', 'sub')), may hold values from -0.375 to 0.375
- near_blocks: bfloat16 [512, 2048, 256], P(('leaf', 'sub')), may hold values from -0.125 to 0.125
- near_source: int32 [512, 8], P(('leaf', 'sub')), may hold values from 0 to 511, as said below
- near_valid: int32 [512, 8], P(('leaf', 'sub')), may hold values from 0 to 1
- leaf_coupling: bfloat16 [512, 64, 2048], P(('leaf', 'sub')), may hold values from -0.125 to 0.125
- leaf_source: int32 [512, 32], P(('leaf', 'sub')), may hold values from 0 to 511, as said below
- leaf_valid: int32 [512, 32], P(('leaf', 'sub')), may hold values from 0 to 1
- parent_transfer: bfloat16 [64, 64, 512], P(('leaf', 'sub')), may hold values from -0.4375 to 0.4375
- parent_coupling: bfloat16 [64, 64, 2048], P(('leaf', 'sub')), may hold values from -0.125 to 0.125
- parent_source: int32 [64, 32], P(('leaf', 'sub')), may hold values from 0 to 63
- parent_valid: int32 [64, 32], P(('leaf', 'sub')), may hold values 0 or 1
- grand_transfer: bfloat16 [8, 64, 512], replicated, may hold values from -0.4375 to 0.4375
- grand_coupling: bfloat16 [8, 64, 1024], P('leaf'), may hold values from -0.1875 to 0.1875
- grand_source: int32 [8, 16], P('leaf'), may hold values from 0 to 7
- grand_valid: int32 [8, 16], P('leaf'), may hold values 0 or 1
Outputs:
- potential: bfloat16 [16, 131072], P(None, ('leaf', 'sub'))
Inputs may be any that keep to these rules, and one draw needn't show every extreme that they name: `leaf_source`: for the 16 leaves of one device (aligned blocks of rows), the slots with leaf_valid = 1 name leaves of any one aligned block of 16 leaves at most 32 times; this bound is reached in every draw. `near_source`: every near source leaf lies within 8 leaves of its target leaf in the curve order; both ends of the reach occur.
All inputs are finite; a program needn't handle non-finite values. No bound on the sum of `parent_valid` or of `grand_valid` on one device may be relied on, other than what follows from the above.
Results may differ from a plain program's by a relative error of at most 0.009.
Values may be sent and summed in bfloat16 or wider, within the bound.
A program may use at most 128 MiB of HBM per device.

v0:
```python
import jax
import jax.numpy as jnp
from jax import lax
from jax.sharding import PartitionSpec as P


def padded_2(cells, sides, width):
    for axis, dim in sides:
        count = lax.axis_size(axis)
        ends = count - 1
        head = lax.slice_in_dim(cells, 0, width, axis=dim)
        tail = lax.slice_in_dim(cells, cells.shape[dim] - width, cells.shape[dim], axis=dim)
        cells = jnp.concatenate(
            [
                lax.ppermute(tail, axis, [(i, (i + 1) % count) for i in range(ends)]),
                cells,
                lax.ppermute(head, axis, [((i + 1) % count, i) for i in range(ends)]),
            ],
            axis=dim,
        )
    return cells


def couple_rows(flat_coefficients, source, valid_slots, blocks, right_sides, rank_width):
    picked = jnp.take(flat_coefficients, source.reshape(-1), axis=0)
    picked = jnp.where(
        valid_slots.reshape(-1)[:, None] == 1, picked, jnp.zeros((), flat_coefficients.dtype)
    )
    picked = picked.reshape(source.shape[0], source.shape[1], right_sides, rank_width)
    coupling_view = blocks.reshape(blocks.shape[0], rank_width, source.shape[1], rank_width)
    return jnp.einsum("tjrb,tajb->tra", picked, coupling_view, preferred_element_type=jnp.float32)


def body(
    densities,
    basis,
    near_blocks,
    near_source,
    near_valid,
    leaf_coupling,
    leaf_source,
    leaf_valid,
    parent_transfer,
    parent_coupling,
    parent_source,
    parent_valid,
    grand_transfer,
    grand_coupling,
    grand_source,
    grand_valid,
):
    right_sides = densities.shape[0]
    owned_leaves, rank_width, leaf_width = basis.shape
    shard_count = lax.axis_size(("leaf", "sub"))
    device_index = lax.axis_index(("leaf", "sub"))
    group_index = lax.axis_index("leaf")
    reach_leaves = owned_leaves // 2
    owned_parents = owned_leaves // 8
    owned_grands = grand_coupling.shape[0]
    row_width = right_sides * rank_width
    blocked = densities.reshape(right_sides, owned_leaves, leaf_width)
    upward = jnp.einsum("rtp,tkp->trk", blocked, basis, preferred_element_type=jnp.float32).astype(
        jnp.bfloat16
    )
    flat_upward = upward.reshape(owned_leaves, row_width)
    children = upward.reshape(owned_parents, 8, right_sides, rank_width)
    parent_view = parent_transfer.reshape(owned_parents, rank_width, 8, rank_width)
    parent_up = jnp.einsum(
        "pcrb,pkcb->prk", children, parent_view, preferred_element_type=jnp.float32
    ).astype(jnp.bfloat16)
    flat_parent = parent_up.reshape(owned_parents, row_width)
    padded = padded_2(densities, ((("leaf", "sub"), 1),), reach_leaves * leaf_width)
    padded = padded.reshape(right_sides, owned_leaves + 2 * reach_leaves, leaf_width)
    local_index = near_source - (device_index * owned_leaves - reach_leaves)
    picked = jnp.take(padded, local_index, axis=1)
    picked = jnp.where(near_valid[None, :, :, None] == 1, picked, jnp.zeros((), jnp.bfloat16))
    picked = picked.reshape(right_sides, owned_leaves, -1)
    near_field = jnp.einsum("rtm,tmq->rtq", picked, near_blocks, preferred_element_type=jnp.float32)
    slot_source = leaf_source.reshape(-1)
    live_slots = leaf_valid.reshape(-1)
    slot_count = slot_source.shape[0]
    capacity = 2 * slot_count // shard_count
    peer_index = slot_source // owned_leaves
    member_leaf = slot_source - peer_index * owned_leaves
    onehot = (
        (peer_index[:, None] == jnp.arange(shard_count, dtype=jnp.int32)[None, :])
        & (live_slots[:, None] == 1)
    ).astype(jnp.int32)
    before = jnp.cumsum(onehot, axis=0) - onehot
    position = jnp.sum(before * onehot, axis=1)
    target_row = jnp.where(live_slots == 1, peer_index, shard_count)
    matches = (
        target_row[:, None, None] == jnp.arange(shard_count, dtype=jnp.int32)[None, :, None]
    ) & (position[:, None, None] == jnp.arange(capacity, dtype=jnp.int32)[None, None, :])
    requested = jnp.sum(jnp.where(matches, member_leaf[:, None, None], 0), axis=0)
    answer = jnp.take(
        flat_upward,
        lax.all_to_all(requested, ("leaf", "sub"), split_axis=0, concat_axis=0, tiled=True),
        axis=0,
    )
    answered = lax.all_to_all(answer, ("leaf", "sub"), split_axis=0, concat_axis=0, tiled=True)
    fetched = answered[
        jnp.where(live_slots == 1, peer_index, 0), jnp.where(live_slots == 1, position, 0)
    ]
    every_parent = lax.all_gather(flat_parent, ("leaf", "sub"), axis=0, tiled=True)
    fetched = jnp.where(live_slots[:, None] == 1, fetched, jnp.zeros((), jnp.bfloat16))
    fetched = fetched.reshape(owned_leaves, leaf_source.shape[1], right_sides, rank_width)
    leaf_view = leaf_coupling.reshape(owned_leaves, rank_width, leaf_source.shape[1], rank_width)
    leaf_far = jnp.einsum("tjrb,tajb->tra", fetched, leaf_view, preferred_element_type=jnp.float32)
    parent_far = couple_rows(
        every_parent, parent_source, parent_valid, parent_coupling, right_sides, rank_width
    )
    first_parent = group_index * (owned_grands * 8)
    own_transfer = lax.dynamic_slice_in_dim(
        grand_transfer, group_index * owned_grands, owned_grands, 0
    )
    group_parents = lax.dynamic_slice_in_dim(every_parent, first_parent, owned_grands * 8, 0)
    group_parents = group_parents.reshape(owned_grands, 8, right_sides, rank_width)
    own_view = own_transfer.reshape(owned_grands, rank_width, 8, rank_width)
    grand_up = jnp.einsum(
        "gcrb,gkcb->grk", group_parents, own_view, preferred_element_type=jnp.float32
    ).astype(jnp.bfloat16)
    every_grand = lax.all_gather(
        grand_up.reshape(owned_grands, row_width), "leaf", axis=0, tiled=True
    )
    grand_total = couple_rows(
        every_grand, grand_source, grand_valid, grand_coupling, right_sides, rank_width
    ).astype(jnp.bfloat16)
    down_view = own_transfer.reshape(owned_grands, rank_width, 8, rank_width)
    down_two = jnp.einsum(
        "grk,gkcb->gcrb", grand_total, down_view, preferred_element_type=jnp.float32
    )
    down_two = down_two.reshape(owned_grands * 8, right_sides, rank_width)
    down_two = lax.dynamic_slice_in_dim(
        down_two, device_index * owned_parents - first_parent, owned_parents, 0
    )
    parent_total = (parent_far + down_two).astype(jnp.bfloat16)
    down_one = jnp.einsum(
        "prk,pkcb->pcrb", parent_total, parent_view, preferred_element_type=jnp.float32
    )
    down_one = down_one.reshape(owned_leaves, right_sides, rank_width)
    leaf_total = (leaf_far + down_one).astype(jnp.bfloat16)
    far_field = jnp.einsum("trk,tkq->rtq", leaf_total, basis, preferred_element_type=jnp.float32)
    summed = (far_field + near_field).astype(jnp.bfloat16)
    return summed.reshape(right_sides, owned_leaves * leaf_width)


def solution(mesh):
    return jax.shard_map(
        body,
        mesh=mesh,
        in_specs=(
            P(None, ("leaf", "sub")),
            P(("leaf", "sub"), None, None),
            P(("leaf", "sub"), None, None),
            P(("leaf", "sub"), None),
            P(("leaf", "sub"), None),
            P(("leaf", "sub"), None, None),
            P(("leaf", "sub"), None),
            P(("leaf", "sub"), None),
            P(("leaf", "sub"), None, None),
            P(("leaf", "sub"), None, None),
            P(("leaf", "sub"), None),
            P(("leaf", "sub"), None),
            P(),
            P("leaf", None, None),
            P("leaf", None),
            P("leaf", None),
        ),
        out_specs=P(None, ("leaf", "sub")),
        check_vma=False,
    )
```

profile of v0, /device:TPU:1, one launch (start us, length us, event | category | flops | bytes accessed | tf_op | source)
XLA Modules:
  0.0 232.1 jit_solution(11413788830165316225)
XLA Ops:
  0.0 0.8 broadcast_compare_fusion
  0.8 0.1 eq.124
  0.9 0.1 eq.134
  0.9 0.8 reshape.498
  1.7 0.8 reshape.499
  2.5 1.2 reduce-window.6
  3.7 0.2 slice_reduce_fusion
  4.0 0.1 fusion.68
  4.1 1.2 select_reduce_fusion
  5.4 7.1 %all-to-all-start = ((s32[32,1,32]{2,1,0:T(1,128)}), s32[32,1,32]{2,1,0:T(1,128)S(1)}, u32[]{:S(2)}, u32[]{:S(2)}) async-start(s32[32,1,32]{2,1,0:T(1,128)} %bitcast.2), calls=%async_computation | async-start | bytes 32768 | tf_op jit(solution)/shard_map/all_to_all | solution.py:98
  12.5 1.5 fusion.110
  14.0 3.3 %collective-permute-start = (bf16[16,2048]{1,0:T(8,128)(2,1)}, bf16[16,2048]{1,0:T(8,128)(2,1)}, u32[]{:S(2)}, u32[]{:S(2)}) collective-permute-start(bf16[16,2048]{1,0:T(8,128)(2,1)} %get-tuple-element.9), channel_id=1, source_target_pairs={{0,1},{1,2},{2,3},{3,4},{4,5},{5,6},{6,7},{7,8},{8,9},{9,10},{10,1... | collective-permute-start | bytes 196616 | tf_op jit(solution)/shard_map/ppermute | solution.py:15
  17.3 4.1 %collective-permute-start.1 = (bf16[16,2048]{1,0:T(8,128)(2,1)}, bf16[16,2048]{1,0:T(8,128)(2,1)}, u32[]{:S(2)}, u32[]{:S(2)}) collective-permute-start(bf16[16,2048]{1,0:T(8,128)(2,1)} %get-tuple-element.10), channel_id=1, source_target_pairs={{1,0},{2,1},{3,2},{4,3},{5,4},{6,5},{7,6},{8,7},{9,8},{10,9},{11,1... | collective-permute-start | bytes 196616 | tf_op jit(solution)/shard_map/ppermute | solution.py:17
  21.4 1.1 convolution_convert_fusion
  22.5 0.1 reshape.502
  22.7 1.1 reshape.506
  23.8 0.1 reshape.522
  23.9 5.4 %gather_fusion = bf16[1024,1024]{1,0:T(8,128)(2,1)} fusion(bf16[16,1024]{1,0:T(8,128)(2,1)S(1)} %reshape.502, s32[1024]{0:T(1024)S(1)} %broadcast_clamp_fusion), kind=kCustom, calls=%fused_computation | custom fusion | bytes 4198400 | tf_op jit(solution)/shard_map/jit(_take)/gather | solution.py:96
  29.2 3.2 %broadcast_select_fusion = bf16[32,32,1024]{2,1,0:T(8,128)(2,1)} fusion(bf16[32,32,1024]{2,1,0:T(8,128)(2,1)} %bitcast.129, pred[32,32]{1,0:T(8,128)(4,1)S(1)} %compare_and_fusion), kind=kLoop, calls=%fused_computation.9 | loop fusion | flops 1048576 | bytes 4195328 | tf_op jit(solution)/shard_map/jit(_take)/select_n | solution.py:96
  32.5 4.3 %all-to-all-start.1 = ((bf16[32,32,1024]{2,1,0:T(8,128)(2,1)}), bf16[32,32,1024]{2,1,0:T(8,128)(2,1)S(1)}, u32[]{:S(2)}, u32[]{:S(2)}) async-start(bf16[32,32,1024]{2,1,0:T(8,128)(2,1)} %broadcast_select_fusion), calls=%async_computation.1 | async-start | bytes 4194304 | tf_op jit(solution)/shard_map/all_to_all | solution.py:101
  36.8 0.0 copy-start.3
  36.8 0.2 fusion.27
  37.0 0.7 eq.138
  37.7 0.7 reshape.503
  38.3 0.1 reshape.561
  38.4 105.7 %all-gather = bf16[32,2,1024]{2,1,0:T(2,128)(2,1)} all-gather(bf16[1,2,1024]{2,1,0:T(2,128)(2,1)S(1)} %reshape.561), channel_id=1, replica_groups=mesh['leaf'=8,'sub'=4] {'leaf','sub'}, dimensions={0}, use_global_device_ids=true | all-gather | bytes 135168 | tf_op jit(solution)/shard_map/all_gather | solution.py:105
  144.2 1.0 reshape.562
  145.2 0.7 reshape.512
  145.9 1.5 constant_dynamic-slice_fusion.1
  147.3 1.6 reshape.510
  149.0 1.1 fusion.30
  150.0 0.1 reshape.563
  150.1 14.3 %all-gather.1 = bf16[8,1,1024]{2,1,0:T(2,128)(2,1)S(1)} all-gather(bf16[1,1,1024]{2,1,0:T(2,128)(2,1)S(1)} %reshape.563), channel_id=1, replica_groups=mesh['leaf'=8,'sub'=4] {'leaf'}, dimensions={0}, use_global_device_ids=true | all-gather | bytes 18432 | tf_op jit(solution)/shard_map/all_gather | solution.py:123
  164.4 0.7 fusion.97
  165.1 0.6 pad_clamp_fusion.1
  165.7 1.3 gather_fusion.3
  167.0 1.5 gather.33
  168.5 1.8 reshape.515
  170.3 0.8 reshape.508
  171.1 1.4 gather_fusion.2
  172.4 1.8 gather.31
  174.3 2.1 reshape.509
  176.3 13.0 %reshape.504 = bf16[16,64,32,64]{3,2,1,0:T(8,128)(2,1)} reshape(bf16[16,64,2048]{2,1,0:T(8,128)(2,1)} %param.21) | data formatting | bytes 8388608 | tf_op jit(solution)/shard_map/reshape | solution.py:108
  189.3 0.1 copy.95
  189.4 0.6 reshape.552
  190.0 0.1 copy.94
  190.1 0.1 broadcast_in_dim.147
  190.2 0.7 broadcast_compare_fusion.1
  190.9 0.1 copy.93
  191.0 0.1 broadcast_in_dim.144
  191.1 1.2 compare_and_fusion.2
  192.3 1.2 compare_bitcast_fusion
  193.5 1.2 compare_and_fusion.3
  194.7 0.7 fusion.90
  195.5 1.7 fusion.43
  197.1 1.9 fusion.41
  199.1 0.9 pad_maximum_fusion
  200.0 1.6 gather_fusion.4
  201.7 2.3 %copy.107 = bf16[16,8,2,8,256]{4,3,1,2,0:T(8,128)(2,1)} copy(bf16[16,8,2,8,256]{4,3,2,1,0:T(8,128)(2,1)} %bitcast.133) | data formatting | bytes 2097152 | tf_op jit(solution)/shard_map/jit(_take)/gather | solution.py:75
  204.0 7.9 %gather_fusion.1 = bf16[512,1024]{1,0:T(8,128)(2,1)} fusion(bf16[32,32,1024]{2,1,0:T(8,128)(2,1)S(1)} %all-to-all-done.1, s32[512]{0:T(512)S(1)} %bitcast.128), kind=kCustom, calls=%fused_computation.1 | custom fusion | bytes 2101248 | tf_op jit(solution)/shard_map/gather | solution.py:102
  211.9 4.0 %gather.29 = bf16[16,32,16,64]{3,2,1,0:T(8,128)(2,1)} reshape(bf16[512,1024]{1,0:T(8,128)(2,1)} %gather_fusion.1) | data formatting | bytes 2097152 | tf_op jit(solution)/shard_map/gather | solution.py:102
  216.0 7.4 %fusion.23 = f32[16,16,256]{2,1,0:T(8,128)S(1)} fusion(bf16[16,64,256]{2,1,0:T(8,128)(2,1)S(1)} %copy-done, f32[16,16,64]{2,1,0:T(8,128)S(1)} %bitcast.144, bf16[16,64,32,64]{3,2,1,0:T(8,128)(2,1)} %reshape.504, bf16[16,32,16,64]{3,2,1,0:T(8,128)(2,1)} %gather.29, pred[16,32]{1,0:T(8,128)(4,1)S(1)} %copy-done.9), kind=kOutput, calls=%fused_computation.17 | convolution fusion | flops 76054528 | bytes 6095360 | tf_op jit(solution)/shard_map/trk,tkq->rtq/dot_general | solution.py:143
  223.4 8.1 %fusion.5 = bf16[16,2,8,256]{3,2,1,0:T(8,128)(2,1)S(1)} fusion(f32[16,16,256]{2,1,0:T(8,128)S(1)} %fusion.23, bf16[16,2048,256]{2,1,0:T(8,128)(2,1)} %param.18, bf16[16,16,2048]{2,0,1:T(8,128)(2,1)S(1)} %bitcast.131, pred[16,2048]{1,0:T(8,128)(4,1)S(1)} %bitcast.137, pred[16,2048]{1,0:T(8,128)(4,1)S(1)} %bitcast.138), kind=kOutput, calls=%fused_computation.13 | convolution fusion | flops 269615104 | bytes 18284544 | tf_op jit(solution)/shard_map/rtm,tmq->rtq/dot_general | solution.py:78
  231.4 0.7 copy.108
  (50 shorter events, 0.3 us)
Async XLA Ops:
  0.0 21.4 %copy-start = (bf16[16,64,256]{2,1,0:T(8,128)(2,1)S(1)}, bf16[16,64,256]{2,1,0:T(8,128)(2,1)}, u32[]{:S(2)}) copy-start(bf16[16,64,256]{2,1,0:T(8,128)(2,1)} %param.17) | copy-start | bytes 1572868
  0.8 36.2 %copy-start.8 = (pred[16,32]{1,0:T(8,128)(4,1)}, pred[16,32]{1,0:T(8,128)(4,1)S(1)}, u32[]{:S(2)}) copy-start(pred[16,32]{1,0:T(8,128)(4,1)S(1)} %broadcast_compare_fusion) | copy-start | bytes 1540
  4.1 17.3 %copy-start.10 = (s32[512]{0:T(512)}, s32[512]{0:T(512)S(1)}, u32[]{:S(2)}) copy-start(s32[512]{0:T(512)S(1)} %fusion.68) | copy-start | bytes 6148
  5.4 18.4 %all-to-all-start = ((s32[32,1,32]{2,1,0:T(1,128)}), s32[32,1,32]{2,1,0:T(1,128)S(1)}, u32[]{:S(2)}, u32[]{:S(2)}) async-start(s32[32,1,32]{2,1,0:T(1,128)} %bitcast.2), calls=%async_computation | async-start | bytes 32768 | tf_op jit(solution)/shard_map/all_to_all | solution.py:98
  14.0 185.1 %collective-permute-start = (bf16[16,2048]{1,0:T(8,128)(2,1)}, bf16[16,2048]{1,0:T(8,128)(2,1)}, u32[]{:S(2)}, u32[]{:S(2)}) collective-permute-start(bf16[16,2048]{1,0:T(8,128)(2,1)} %get-tuple-element.9), channel_id=1, source_target_pairs={{0,1},{1,2},{2,3},{3,4},{4,5},{5,6},{6,7},{7,8},{8,9},{9,10},{10,1... | collective-permute-start | bytes 196616 | tf_op jit(solution)/shard_map/ppermute | solution.py:15
  17.3 181.8 %collective-permute-start.1 = (bf16[16,2048]{1,0:T(8,128)(2,1)}, bf16[16,2048]{1,0:T(8,128)(2,1)}, u32[]{:S(2)}, u32[]{:S(2)}) collective-permute-start(bf16[16,2048]{1,0:T(8,128)(2,1)} %get-tuple-element.10), channel_id=1, source_target_pairs={{1,0},{2,1},{3,2},{4,3},{5,4},{6,5},{7,6},{8,7},{9,8},{10,9},{11,1... | collective-permute-start | bytes 196616 | tf_op jit(solution)/shard_map/ppermute | solution.py:17
  32.5 5.2 %copy-start.6 = (s32[16,32]{1,0:T(8,128)S(1)}, s32[16,32]{1,0:T(8,128)}, u32[]{:S(2)}) copy-start(s32[16,32]{1,0:T(8,128)} %param.22) | copy-start | bytes 6148
  32.5 171.6 %all-to-all-start.1 = ((bf16[32,32,1024]{2,1,0:T(8,128)(2,1)}), bf16[32,32,1024]{2,1,0:T(8,128)(2,1)S(1)}, u32[]{:S(2)}, u32[]{:S(2)}) async-start(bf16[32,32,1024]{2,1,0:T(8,128)(2,1)} %broadcast_select_fusion), calls=%async_computation.1 | async-start | bytes 4194304 | tf_op jit(solution)/shard_map/all_to_all | solution.py:101
  36.8 137.5 %copy-start.3 = (bf16[2,64,2048]{2,1,0:T(8,128)(2,1)S(1)}, bf16[2,64,2048]{2,1,0:T(8,128)(2,1)}, u32[]{:S(2)}) copy-start(bf16[2,64,2048]{2,1,0:T(8,128)(2,1)} %param.25) | copy-start | bytes 1572868
  176.3 13.0 %copy-start.12 = (s32[16,8]{0,1:T(8,128)S(1)}, s32[16,8]{0,1:T(8,128)}, u32[]{:S(2)}) copy-start(s32[16,8]{0,1:T(8,128)} %param.19) | copy-start | bytes 1540
  176.3 18.4 %copy-start.11 = (s32[512]{0:T(512)S(1)}, s32[512]{0:T(512)}, u32[]{:S(2)}) copy-start(s32[512]{0:T(512)} %copy-done.10) | copy-start | bytes 6148
  176.3 19.1 %copy-start.4 = (bf16[64,8,64]{2,1,0:T(8,128)(2,1)S(1)}, bf16[64,8,64]{2,1,0:T(8,128)(2,1)}, u32[]{:S(2)}) copy-start(bf16[64,8,64]{2,1,0:T(8,128)(2,1)} %reshape.510) | copy-start | bytes 196612
  176.3 19.1 %copy-start.5 = (bf16[64,16,64]{2,1,0:T(8,128)(2,1)S(1)}, bf16[64,16,64]{2,1,0:T(8,128)(2,1)}, u32[]{:S(2)}) copy-start(bf16[64,16,64]{2,1,0:T(8,128)(2,1)} %reshape.515) | copy-start | bytes 393220
  176.3 19.1 %copy-start.7 = (bf16[16,16,64]{2,1,0:T(8,128)(2,1)S(1)}, bf16[16,16,64]{2,1,0:T(8,128)(2,1)}, u32[]{:S(2)}) copy-start(bf16[16,16,64]{2,1,0:T(8,128)(2,1)} %gather.33) | copy-start | bytes 98308
  189.3 9.8 %copy-start.2 = (bf16[16,4096]{1,0:T(8,128)(2,1)S(1)}, bf16[16,4096]{1,0:T(8,128)(2,1)}, u32[]{:S(2)}) copy-start(bf16[16,4096]{1,0:T(8,128)(2,1)} %param.16) | copy-start | bytes 393220
  190.0 9.0 %copy-start.13 = (s32[128]{0:T(128)S(1)}, s32[128]{0:T(128)}, u32[]{:S(2)}) copy-start(s32[128]{0:T(128)} %reshape.552) | copy-start | bytes 1540
  211.9 4.0 %copy-start.9 = (pred[16,32]{1,0:T(8,128)(4,1)S(1)}, pred[16,32]{1,0:T(8,128)(4,1)}, u32[]{:S(2)}) copy-start(pred[16,32]{1,0:T(8,128)(4,1)} %copy-done.8) | copy-start | bytes 1540
  216.0 7.4 %copy-start.1 = (bf16[16,8,2,8,256]{4,3,1,2,0:T(8,128)(2,1)S(1)}, bf16[16,8,2,8,256]{4,3,1,2,0:T(8,128)(2,1)}, u32[]{:S(2)}) copy-start(bf16[16,8,2,8,256]{4,3,1,2,0:T(8,128)(2,1)} %copy.107) | copy-start | bytes 3145732
where the time goes:
time: 234 us; the launch traced here: 232 us
  blocking collectives  120 us (51%)
  local copies, waits for them, and re-layouts  57.9 us (25%)
  matrix products  21.4 us (9%)
  starting transfers between devices  18.8 us (8%)
  other arithmetic  13.8 us (6%)
    all_gather x1, blocking collectives, body(): lax.all_gather(flat_parent, ('leaf', 'sub'), axis=0, tiled=True)  106 us
    all_gather x1, blocking collectives, body(): lax.all_gather(grand_up.reshape(owned_grands, row_width), 'leaf', axis=0,...  14.3 us
    reshape x1, local copies, waits for them, and re-layouts, body(): leaf_coupling.reshape(owned_leaves, rank_width, leaf_source.shape[1], ran...  13 us
    gather x2, local copies, waits for them, and re-layouts, body(): answered[jnp.where(live_slots == 1, peer_index, 0), jnp.where(live_slots...  11.9 us
    dot_general x1, matrix products, body(): jnp.einsum('rtm,tmq->rtq', picked, near_blocks, preferred_element_type=jn...  8.06 us
    dot_general x1, matrix products, body(): jnp.einsum('trk,tkq->rtq', leaf_total, basis, preferred_element_type=jnp....  7.4 us
    all_to_all x1, starting transfers between devices, body(): lax.all_to_all(requested, ('leaf', 'sub'), split_axis=0, concat_axis=0, t...  7.1 us
    gather x4, local copies, waits for them, and re-layouts, couple_rows(): picked = jnp.take(flat_coefficients, source.reshape(-1), axis=0)  6.02 us
  transfers between devices with their start and end apart: 4, of which 0 were waited for; matrix products, arithmetic and copies ran while one was open for 26% of the time, Pallas kernels for 0%

commit v1 on v0

v1 whole, which is shorter than its diff:
```python
import functools

import jax
import jax.numpy as jnp
from jax import lax
from jax.experimental import pallas as pl
from jax.experimental.pallas import tpu as pltpu
from jax.sharding import PartitionSpec as P

BF16 = jnp.bfloat16
F32 = jnp.float32
CORES = 2
LANES = 128


def dot_nt(a, b):
    return lax.dot_general(a, b, (((1,), (1,)), ((), ())), preferred_element_type=F32)


def dot_nn(a, b):
    return lax.dot_general(a, b, (((1,), (0,)), ((), ())), preferred_element_type=F32)


def fused_kernel(
    groups,
    subs,
    near_source,
    near_valid,
    leaf_source,
    leaf_valid,
    parent_source,
    parent_valid,
    grand_source,
    grand_valid,
    densities,
    basis,
    near_blocks,
    leaf_coupling,
    parent_transfer,
    parent_coupling,
    grand_transfer,
    grand_coupling,
    out,
    padded,
    slabs,
    basis_v,
    near_v,
    coupling_v,
    transfer_v,
    parent_coupling_v,
    grand_transfer_v,
    grand_coupling_v,
    table,
    leaf_rows,
    parent_rows,
    grand_rows,
    near_sum,
    leaf_far,
    load_sem,
    near_sem,
    coupling_sem,
    halo_send,
    halo_recv,
    line_send,
    line_recv,
    plane_send,
    plane_recv,
    twin_send,
    twin_recv,
):
    rs = densities.shape[0]
    pairs, pair_rank, width = basis.shape
    leaves = 2 * pairs
    rank = pair_rank // 2
    reach = leaves // 2
    near_slots = near_source.shape[1]
    leaf_slots = leaf_source.shape[1]
    grand_slots = grand_source.shape[1]
    total_devices = groups * subs
    total_leaves = total_devices * leaves
    total_parents = total_devices * 2
    chips = groups // CORES
    low = lax.broadcasted_iota(jnp.int32, (rs, LANES), 1) < rank

    group = lax.axis_index("leaf")
    sub = lax.axis_index("sub")
    me = group * subs + sub
    chip = group // CORES
    core = group % CORES
    following = (me + 1) % total_devices
    previous = (me + total_devices - 1) % total_devices
    following = (following // subs, following % subs)
    previous = (previous // subs, previous % subs)
    twin = (chip * CORES + (1 - core), sub)

    def line(i):
        return (group, (sub + i) % subs)

    def plane(k):
        return (((chip + k) % chips) * CORES + core, sub)

    reach_width = reach * width
    own_width = leaves * width
    loads = [
        pltpu.make_async_copy(
            densities, padded.at[:, reach_width : reach_width + own_width], load_sem.at[0]
        ),
        pltpu.make_async_copy(basis, basis_v, load_sem.at[1]),
        pltpu.make_async_copy(parent_transfer, transfer_v, load_sem.at[2]),
        pltpu.make_async_copy(grand_transfer, grand_transfer_v, load_sem.at[3]),
        pltpu.make_async_copy(parent_coupling, parent_coupling_v, load_sem.at[4]),
        pltpu.make_async_copy(grand_coupling, grand_coupling_v, load_sem.at[5]),
    ]

    def near_load(t):
        return pltpu.make_async_copy(near_blocks.at[t], near_v.at[t], near_sem.at[t])

    def coupling_load(i):
        return pltpu.make_async_copy(leaf_coupling.at[i], coupling_v.at[i], coupling_sem.at[i])

    for load in loads[:3]:
        load.start()

    barrier = pltpu.get_barrier_semaphore()
    partners = [following, previous, twin]
    partners += [line(i) for i in range(1, subs)] + [plane(k) for k in range(1, chips)]
    for partner in partners:
        pl.semaphore_signal(
            barrier, inc=1, device_id=partner, device_id_type=pl.DeviceIdType.MESH
        )

    lax.fori_loop(0, leaves, lambda t, c: (near_load(t).start(), c)[1], 0)
    for load in loads[3:]:
        load.start()
    lax.fori_loop(0, pairs, lambda i, c: (coupling_load(i).start(), c)[1], 0)

    slabs[leaves + 2 * reach] = jnp.zeros((rs, width), BF16)
    leaf_rows[total_leaves] = jnp.zeros((rs, LANES), BF16)
    parent_rows[total_parents] = jnp.zeros((rs, LANES), BF16)
    grand_rows[groups] = jnp.zeros((rs, LANES), BF16)

    pl.semaphore_wait(barrier, len(partners))

    def remote(src, dst, send, recv, device):
        return pltpu.make_async_remote_copy(
            src_ref=src,
            dst_ref=dst,
            send_sem=send,
            recv_sem=recv,
            device_id=device,
            device_id_type=pl.DeviceIdType.MESH,
        )

    halo = [
        remote(
            densities.at[:, own_width - reach_width :],
            padded.at[:, :reach_width],
            halo_send.at[0],
            halo_recv.at[0],
            following,
        ),
        remote(
            densities.at[:, :reach_width],
            padded.at[:, reach_width + own_width :],
            halo_send.at[1],
            halo_recv.at[1],
            previous,
        ),
    ]
    for copy in halo:
        copy.start()

    for load in loads[:3]:
        load.wait()

    def tile_of(both):
        return jnp.where(low, both[:rs], both[rs:])

    own = table.at[group, sub]
    tiles = []
    for i in range(pairs):
        start = reach_width + 2 * i * width
        two = jnp.concatenate(
            [padded[:, start : start + width], padded[:, start + width : start + 2 * width]], axis=0
        )
        tile = tile_of(dot_nt(two, basis_v[i])).astype(BF16)
        own[i] = tile
        tiles.append(tile)
    children = jnp.concatenate(
        [jnp.concatenate(tiles[:4], axis=1), jnp.concatenate(tiles[4:], axis=1)], axis=0
    )
    own[pairs] = tile_of(dot_nt(children, transfer_v[...])).astype(BF16)

    def line_copy(i):
        block = table.at[group, sub]
        return remote(block, block, line_send.at[i], line_recv.at[i], line(i))

    def plane_copy(i, k):
        block = table.at[group, (sub + subs - i) % subs]
        return remote(block, block, plane_send.at[i, k], plane_recv.at[i, k], plane(k))

    def twin_copy(i, k):
        block = table.at[((chip + chips - k) % chips) * CORES + core, (sub + subs - i) % subs]
        return remote(block, block, twin_send.at[i, k], twin_recv.at[i, k], twin)

    def spread(i):
        if i > 0:
            line_copy(i).wait_recv()
        for k in range(1, chips):
            plane_copy(i, k).start()
        twin_copy(i, 0).start()

    def pass_on(i):
        for k in range(1, chips):
            plane_copy(i, k).wait_recv()
            twin_copy(i, k).start()

    for i in range(1, subs):
        line_copy(i).start()
    spread(0)

    def choose(valid, source, missing):
        return missing + valid * (source - missing)

    base = me * leaves - reach

    def near_step(t, carry):
        near_load(t).wait()
        total = jnp.zeros((rs, width), F32)
        for j in range(near_slots):
            place = choose(near_valid[t, j], near_source[t, j] - base, leaves + 2 * reach)
            total += dot_nn(slabs[place], near_v[t, j * width : (j + 1) * width, :])
        near_sum[:, pl.ds(pl.multiple_of(t * width, width), width)] = total
        return carry

    for copy in halo:
        copy.wait()
    for i in range(leaves + 2 * reach):
        slabs[i] = padded[:, i * width : (i + 1) * width]
    cuts = [0]
    for i in range(1, subs):
        cuts.append(leaves * i // (2 * subs) + 1)
        lax.fori_loop(cuts[-2], cuts[-1], near_step, 0)
        spread(i)
    for i in range(subs):
        cuts.append(leaves if i == subs - 1 else cuts[-1] + (leaves - cuts[-1]) // (subs - i))
        lax.fori_loop(cuts[-2], cuts[-1], near_step, 0)
        pass_on(i)
    for i in range(subs):
        for k in range(chips):
            twin_copy(i, k).wait_recv()

    def duplicate(tile):
        turned = jnp.concatenate([tile[:, rank:], tile[:, :rank]], axis=1)
        return jnp.where(low, tile, turned), jnp.where(low, turned, tile)

    def unpack(d, carry):
        g, s = d // subs, d % subs
        for i in range(pairs):
            first, second = duplicate(table[g, s, i])
            leaf_rows[d * leaves + 2 * i] = first
            leaf_rows[d * leaves + 2 * i + 1] = second
        first, second = duplicate(table[g, s, pairs])
        parent_rows[2 * d] = first
        parent_rows[2 * d + 1] = second
        return carry

    lax.fori_loop(0, total_devices, unpack, 0)

    def gather(rows, source, valid, t, slots, missing):
        parts = []
        for j in range(0, slots, 2):
            a = rows[choose(valid[t, j], source[t, j], missing)]
            b = rows[choose(valid[t, j + 1], source[t, j + 1], missing)]
            parts.append(jnp.where(low, a, b))
        return jnp.concatenate(parts, axis=1)

    for load in loads[3:]:
        load.wait()

    def lift(g, carry):
        up = jnp.concatenate([table[g, s, pairs] for s in range(subs)], axis=1)
        up = dot_nt(up, grand_transfer_v[g]).astype(BF16)
        grand_rows[g] = jnp.concatenate([up, up], axis=1)
        return carry

    lax.fori_loop(0, groups, lift, 0)
    picked = gather(grand_rows, grand_source, grand_valid, 0, grand_slots, groups)
    grand_total = dot_nt(picked, grand_coupling_v[0]).astype(BF16)
    parent_lanes = pl.ds(pl.multiple_of(sub * LANES, LANES), LANES)
    down_two = dot_nn(grand_total, grand_transfer_v[group, :, parent_lanes])

    def pair_far(rows, source, valid, t, missing, blocks):
        two = jnp.concatenate(
            [gather(rows, source, valid, t + h, leaf_slots, missing) for h in range(2)], axis=0
        )
        return tile_of(dot_nt(two, blocks))

    parent_far = pair_far(
        parent_rows, parent_source, parent_valid, 0, total_parents, parent_coupling_v[...]
    )
    parent_total = (parent_far + down_two).astype(BF16)
    nothing = jnp.zeros((rs, LANES), BF16)

    def split(tile):
        return jnp.concatenate(
            [jnp.where(low, tile, nothing), jnp.where(low, nothing, tile)], axis=0
        )

    down_one = dot_nn(split(parent_total), transfer_v[...])
    half = pairs // 2
    for i in range(pairs):
        row = (i // half) * rs
        lane = (i % half) * LANES
        leaf_far[i] = down_one[row : row + rs, lane : lane + LANES]

    def leaf_step(i, carry):
        coupling_load(i).wait()
        far = pair_far(leaf_rows, leaf_source, leaf_valid, 2 * i, total_leaves, coupling_v[i])
        leaf_total = (far + leaf_far[i]).astype(BF16)
        both = dot_nn(split(leaf_total), basis_v[i])
        for h in range(2):
            lanes = pl.ds(pl.multiple_of((2 * i + h) * width, width), width)
            out[:, lanes] = (both[h * rs : (h + 1) * rs] + near_sum[:, lanes]).astype(BF16)
        return carry

    lax.fori_loop(0, pairs, leaf_step, 0)

    for i in range(1, subs):
        line_copy(i).wait_send()
    for i in range(subs):
        for k in range(chips):
            if k > 0:
                plane_copy(i, k).wait_send()
            twin_copy(i, k).wait_send()


def body(
    groups,
    subs,
    densities,
    basis,
    near_blocks,
    near_source,
    near_valid,
    leaf_coupling,
    leaf_source,
    leaf_valid,
    parent_transfer,
    parent_coupling,
    parent_source,
    parent_valid,
    grand_transfer,
    grand_coupling,
    grand_source,
    grand_valid,
):
    rs = densities.shape[0]
    leaves, rank, width = basis.shape
    pairs = leaves // 2
    devices = groups * subs
    chips = groups // CORES
    basis = basis.reshape(pairs, 2 * rank, width)
    leaf_coupling = leaf_coupling.reshape(pairs, 2 * rank, leaf_coupling.shape[2])
    parent_transfer = parent_transfer.reshape(2 * rank, parent_transfer.shape[2])
    parent_coupling = parent_coupling.reshape(2 * rank, parent_coupling.shape[2])
    smem = pl.BlockSpec(memory_space=pltpu.SMEM)
    anywhere = pl.BlockSpec(memory_space=pl.ANY)
    dma = pltpu.SemaphoreType.DMA
    return pl.pallas_call(
        functools.partial(fused_kernel, groups, subs),
        out_shape=jax.ShapeDtypeStruct(densities.shape, BF16),
        in_specs=[smem] * 8 + [anywhere] * 8,
        out_specs=pl.BlockSpec(memory_space=pltpu.VMEM),
        scratch_shapes=[
            pltpu.VMEM((rs, 2 * leaves * width), BF16),
            pltpu.VMEM((2 * leaves + 1, rs, width), BF16),
            pltpu.VMEM(basis.shape, BF16),
            pltpu.VMEM(near_blocks.shape, BF16),
            pltpu.VMEM(leaf_coupling.shape, BF16),
            pltpu.VMEM(parent_transfer.shape, BF16),
            pltpu.VMEM(parent_coupling.shape, BF16),
            pltpu.VMEM(grand_transfer.shape, BF16),
            pltpu.VMEM(grand_coupling.shape, BF16),
            pltpu.VMEM((groups, subs, pairs + 1, rs, LANES), BF16),
            pltpu.VMEM((devices * leaves + 1, rs, LANES), BF16),
            pltpu.VMEM((devices * 2 + 1, rs, LANES), BF16),
            pltpu.VMEM((groups + 1, rs, LANES), BF16),
            pltpu.VMEM((rs, leaves * width), F32),
            pltpu.VMEM((pairs, rs, LANES), F32),
            dma((6,)),
            dma((leaves,)),
            dma((pairs,)),
            dma((2,)),
            dma((2,)),
            dma((subs,)),
            dma((subs,)),
            dma((subs, chips)),
            dma((subs, chips)),
            dma((subs, chips)),
            dma((subs, chips)),
        ],
        compiler_params=pltpu.CompilerParams(
            collective_id=0, has_side_effects=True, vmem_limit_bytes=52 * 1024 * 1024
        ),
        cost_estimate=pl.CostEstimate(
            flops=2 * rs * near_blocks.size, bytes_accessed=2 * near_blocks.size, transcendentals=0
        ),
    )(
        near_source,
        near_valid,
        leaf_source,
        leaf_valid,
        parent_source,
        parent_valid,
        grand_source,
        grand_valid,
        densities,
        basis,
        near_blocks,
        leaf_coupling,
        parent_transfer,
        parent_coupling,
        grand_transfer,
        grand_coupling,
    )


def solution(mesh):
    both = ("leaf", "sub")
    return jax.shard_map(
        functools.partial(body, mesh.shape["leaf"], mesh.shape["sub"]),
        mesh=mesh,
        in_specs=(
            P(None, both),
            P(both, None, None),
            P(both, None, None),
            P(both, None),
            P(both, None),
            P(both, None, None),
            P(both, None),
            P(both, None),
            P(both, None, None),
            P(both, None, None),
            P(both, None),
            P(both, None),
            P(),
            P("leaf", None, None),
            P("leaf", None),
            P("leaf", None),
        ),
        out_specs=P(None, both),
        check_vma=False,
    )
```

time: 234 us -> 40.3 us (0.17)
  blocking collectives: 120 us -> 0 us
  local copies, waits for them, and re-layouts: 57.9 us -> 11 us
  Pallas kernels: 0 us -> 28.8 us
  matrix products: 21.4 us -> 0 us
  starting transfers between devices: 18.8 us -> 0 us
  other arithmetic: 13.8 us -> 0 us
    all_gather x2 -> x0, blocking collectives: 120 us -> none  [the longest x1 106 us: body(): lax.all_gather(flat_parent, ('leaf', 'sub'), axis=0, tiled=True)]
    pallas_call x0 -> x1, Pallas kernels: none -> 28.8 us  [body(): pl.pallas_call(functools.partial(fused_kernel, groups, subs), out_shape=j...]
    gather x9 -> x0, local copies, waits for them, and re-layouts: 27.3 us -> none  [the longest x2 11.9 us: body(): answered[jnp.where(live_slots == 1, peer_index, 0), jnp.where(live_slots...]
    dot_general x7 -> x0, matrix products: 21.4 us -> none  [the longest x1 8.06 us: body(): jnp.einsum('rtm,tmq->rtq', picked, near_blocks, preferred_element_type=jn...]
    reshape x10 -> x0, local copies, waits for them, and re-layouts: 19.9 us -> none  [the longest x1 13 us: body(): leaf_coupling.reshape(owned_leaves, rank_width, leaf_source.shape[1], ran...]
    all_to_all x2 -> x0, starting transfers between devices: 11.4 us -> none  [the longest x1 7.1 us: body(): lax.all_to_all(requested, ('leaf', 'sub'), split_axis=0, concat_axis=0, t...]
    unnamed x34 -> x25, local copies, waits for them, and re-layouts: 1.23 us -> 11 us
    ppermute x2 -> x0, starting transfers between devices: 7.35 us -> none  [the longest x1 4.06 us: padded_2(): lax.ppermute(head, axis, [((i + 1) % count, i) for i in range(ends)])]
  transfers between devices with their start and end apart: 4 -> 0, of which waited for: 0 -> 0; matrix products, arithmetic and copies ran while one was open for 26% -> 0% of each run, Pallas kernels for 0% -> 0%
where the time goes in v1:
time: 40.3 us; the launch traced here: 39.8 us
  Pallas kernels  28.8 us (71%)
  local copies, waits for them, and re-layouts  11 us (27%)
    pallas_call x1, Pallas kernels, body(): pl.pallas_call(functools.partial(fused_kernel, groups, subs), out_shape=j...  28.8 us
    unnamed x25, local copies, waits for them, and re-layouts  11 us

profile of v1, /device:TPU:1, one launch (start us, length us, event | category | flops | bytes accessed | tf_op | source)
XLA Modules:
  0.0 39.8 jit_solution(11422655666964104126)
XLA Ops:
  0.0 0.8 %copy.17.near_source = s32[16,8]{1,0:T(8,128)S(1)} copy(s32[16,8]{0,1:T(8,128)} %param.19) | data formatting | bytes 1024 | tf_op args[3]
  0.8 0.8 %copy.18.near_valid = s32[16,8]{1,0:T(8,128)S(1)} copy(s32[16,8]{0,1:T(8,128)} %param.20) | data formatting | bytes 1024 | tf_op args[4]
  1.5 0.0 copy-start
  1.5 1.0 %copy-done = bf16[16,64,256]{2,1,0:T(8,128)(2,1)S(1)} copy-done((bf16[16,64,256]{2,1,0:T(8,128)(2,1)S(1)}, bf16[16,64,256]{2,1,0:T(8,128)(2,1)}, u32[]{:S(2)}) %copy-start) | copy-done | bytes 524312
  2.6 0.0 copy-start.1
  2.6 1.0 %copy-done.1 = bf16[2,64,2048]{2,1,0:T(8,128)(2,1)S(1)} copy-done((bf16[2,64,2048]{2,1,0:T(8,128)(2,1)S(1)}, bf16[2,64,2048]{2,1,0:T(8,128)(2,1)}, u32[]{:S(2)}) %copy-start.1) | copy-done | bytes 524312
  3.6 0.0 copy-start.2
  3.6 0.9 %copy-done.2 = bf16[16,4096]{1,0:T(8,128)(2,1)S(1)} copy-done((bf16[16,4096]{1,0:T(8,128)(2,1)S(1)}, bf16[16,4096]{1,0:T(8,128)(2,1)}, u32[]{:S(2)}) %copy-start.2) | copy-done | bytes 131096
  4.5 0.0 copy-start.3
  4.5 0.9 %copy-done.3 = bf16[2,64,512]{2,1,0:T(8,128)(2,1)S(1)} copy-done((bf16[2,64,512]{2,1,0:T(8,128)(2,1)S(1)}, bf16[2,64,512]{2,1,0:T(8,128)(2,1)}, u32[]{:S(2)}) %copy-start.3) | copy-done | bytes 131096
  5.4 0.0 copy-start.4
  5.4 0.9 %copy-done.4 = bf16[1,64,1024]{2,1,0:T(8,128)(2,1)S(1)} copy-done((bf16[1,64,1024]{2,1,0:T(8,128)(2,1)S(1)}, bf16[1,64,1024]{2,1,0:T(8,128)(2,1)}, u32[]{:S(2)}) %copy-start.4) | copy-done | bytes 131096
  6.3 0.0 copy-start.5
  6.3 0.7 %copy-done.5 = s32[16,32]{1,0:T(8,128)S(1)} copy-done((s32[16,32]{1,0:T(8,128)S(1)}, s32[16,32]{1,0:T(8,128)}, u32[]{:S(2)}) %copy-start.5) | copy-done | bytes 2072
  7.0 0.0 copy-start.6
  7.0 0.7 %copy-done.6 = s32[16,32]{1,0:T(8,128)S(1)} copy-done((s32[16,32]{1,0:T(8,128)S(1)}, s32[16,32]{1,0:T(8,128)}, u32[]{:S(2)}) %copy-start.6) | copy-done | bytes 2072
  7.7 0.0 copy-start.7
  7.7 0.7 %copy-done.7 = s32[2,32]{1,0:T(2,128)S(1)} copy-done((s32[2,32]{1,0:T(2,128)S(1)}, s32[2,32]{1,0:T(2,128)}, u32[]{:S(2)}) %copy-start.7) | copy-done | bytes 280
  8.4 0.0 copy-start.8
  8.4 0.7 %copy-done.8 = s32[2,32]{1,0:T(2,128)S(1)} copy-done((s32[2,32]{1,0:T(2,128)S(1)}, s32[2,32]{1,0:T(2,128)}, u32[]{:S(2)}) %copy-start.8) | copy-done | bytes 280
  9.1 0.0 copy-start.9
  9.1 0.7 %copy-done.9 = s32[1,16]{1,0:T(1,128)S(1)} copy-done((s32[1,16]{1,0:T(1,128)S(1)}, s32[1,16]{1,0:T(1,128)}, u32[]{:S(2)}) %copy-start.9) | copy-done | bytes 88
  9.7 0.0 copy-start.10
  9.7 0.7 %copy-done.10 = s32[1,16]{1,0:T(1,128)S(1)} copy-done((s32[1,16]{1,0:T(1,128)S(1)}, s32[1,16]{1,0:T(1,128)}, u32[]{:S(2)}) %copy-start.10) | copy-done | bytes 88
  10.4 28.8 %shard_map.154 = bf16[16,4096]{1,0:T(8,128)(2,1)S(1)} custom-call(s32[16,8]{1,0:T(8,128)S(1)} %copy.17.near_source, s32[16,8]{1,0:T(8,128)S(1)} %copy.18.near_valid, s32[16,32]{1,0:T(8,128)S(1)} %copy-done.5, s32[16,32]{1,0:T(8,128)S(1)} %copy-done.6, s32[2,32]{1,0:T(2,128)S(1)} %copy-done.7, s32[2,32]{1,0:T(2,128)S(1)} %copy-done.8, s32[1,16]{1,0:T(1,128)S(1)} %copy-done.9, ...), custom_call_target="tpu_custom_call" | custom-call | flops 268435456 | bytes 16777216 | tf_op jit(solution)/shard_map/pallas_call | solution.py:370
  39.2 0.7 %copy.20 = bf16[16,4096]{1,0:T(8,128)(2,1)} copy(bf16[16,4096]{1,0:T(8,128)(2,1)S(1)} %shard_map.154) | data formatting | bytes 262144
Async XLA Ops:
  1.5 1.0 %copy-start = (bf16[16,64,256]{2,1,0:T(8,128)(2,1)S(1)}, bf16[16,64,256]{2,1,0:T(8,128)(2,1)}, u32[]{:S(2)}) copy-start(bf16[16,64,256]{2,1,0:T(8,128)(2,1)} %param.17) | copy-start | bytes 1572868
  2.6 1.0 %copy-start.1 = (bf16[2,64,2048]{2,1,0:T(8,128)(2,1)S(1)}, bf16[2,64,2048]{2,1,0:T(8,128)(2,1)}, u32[]{:S(2)}) copy-start(bf16[2,64,2048]{2,1,0:T(8,128)(2,1)} %param.25) | copy-start | bytes 1572868
  3.6 0.9 %copy-start.2 = (bf16[16,4096]{1,0:T(8,128)(2,1)S(1)}, bf16[16,4096]{1,0:T(8,128)(2,1)}, u32[]{:S(2)}) copy-start(bf16[16,4096]{1,0:T(8,128)(2,1)} %densities.1) | copy-start | bytes 393220
  4.5 0.9 %copy-start.3 = (bf16[2,64,512]{2,1,0:T(8,128)(2,1)S(1)}, bf16[2,64,512]{2,1,0:T(8,128)(2,1)}, u32[]{:S(2)}) copy-start(bf16[2,64,512]{2,1,0:T(8,128)(2,1)} %param.24) | copy-start | bytes 393220
  5.4 0.9 %copy-start.4 = (bf16[1,64,1024]{2,1,0:T(8,128)(2,1)S(1)}, bf16[1,64,1024]{2,1,0:T(8,128)(2,1)}, u32[]{:S(2)}) copy-start(bf16[1,64,1024]{2,1,0:T(8,128)(2,1)} %grand_coupling.1) | copy-start | bytes 393220
  6.3 0.7 %copy-start.5 = (s32[16,32]{1,0:T(8,128)S(1)}, s32[16,32]{1,0:T(8,128)}, u32[]{:S(2)}) copy-start(s32[16,32]{1,0:T(8,128)} %leaf_source.1) | copy-start | bytes 6148
  7.0 0.7 %copy-start.6 = (s32[16,32]{1,0:T(8,128)S(1)}, s32[16,32]{1,0:T(8,128)}, u32[]{:S(2)}) copy-start(s32[16,32]{1,0:T(8,128)} %leaf_valid.1) | copy-start | bytes 6148
  7.7 0.7 %copy-start.7 = (s32[2,32]{1,0:T(2,128)S(1)}, s32[2,32]{1,0:T(2,128)}, u32[]{:S(2)}) copy-start(s32[2,32]{1,0:T(2,128)} %parent_source.1) | copy-start | bytes 772
  8.4 0.7 %copy-start.8 = (s32[2,32]{1,0:T(2,128)S(1)}, s32[2,32]{1,0:T(2,128)}, u32[]{:S(2)}) copy-start(s32[2,32]{1,0:T(2,128)} %parent_valid.1) | copy-start | bytes 772
  9.1 0.7 %copy-start.9 = (s32[1,16]{1,0:T(1,128)S(1)}, s32[1,16]{1,0:T(1,128)}, u32[]{:S(2)}) copy-start(s32[1,16]{1,0:T(1,128)} %grand_source.1) | copy-start | bytes 196
  9.7 0.7 %copy-start.10 = (s32[1,16]{1,0:T(1,128)S(1)}, s32[1,16]{1,0:T(1,128)}, u32[]{:S(2)}) copy-start(s32[1,16]{1,0:T(1,128)} %grand_valid.1) | copy-start | bytes 196

commit v2 on v1

--- a/solution.py
+++ b/solution.py
@@ -24,14 +24,10 @@
 def fused_kernel(
     groups,
     subs,
-    near_source,
-    near_valid,
-    leaf_source,
-    leaf_valid,
-    parent_source,
-    parent_valid,
-    grand_source,
-    grand_valid,
+    *refs,
+):
+    lists, refs = refs[:8], refs[8:]
+    (
     densities,
     basis,
     near_blocks,
@@ -55,7 +51,6 @@
     parent_rows,
     grand_rows,
     near_sum,
-    leaf_far,
     load_sem,
     near_sem,
     coupling_sem,
@@ -67,15 +62,19 @@
     plane_recv,
     twin_send,
     twin_recv,
-):
+    list_sem,
+    place_sem,
+    ), refs = refs[:36], refs[36:]
+    lists_v, places_v, places = refs[:8], refs[8:12], refs[12:]
+    near_place, leaf_place, parent_place, grand_place = places
     rs = densities.shape[0]
     pairs, pair_rank, width = basis.shape
     leaves = 2 * pairs
     rank = pair_rank // 2
     reach = leaves // 2
-    near_slots = near_source.shape[1]
-    leaf_slots = leaf_source.shape[1]
-    grand_slots = grand_source.shape[1]
+    near_slots = lists[0].shape[0]
+    leaf_slots = lists[2].shape[1]
+    grand_slots = lists[6].shape[1]
     total_devices = groups * subs
     total_leaves = total_devices * leaves
     total_parents = total_devices * 2
@@ -112,13 +111,21 @@
         pltpu.make_async_copy(grand_coupling, grand_coupling_v, load_sem.at[5]),
     ]
 
-    def near_load(t):
-        return pltpu.make_async_copy(near_blocks.at[t], near_v.at[t], near_sem.at[t])
+    list_loads = [
+        pltpu.make_async_copy(lists[n], lists_v[n], list_sem.at[n]) for n in range(8)
+    ]
+    place_loads = [
+        pltpu.make_async_copy(places_v[n], places[n], place_sem.at[n]) for n in range(4)
+    ]
+
+    def near_load(i):
+        both = pl.ds(2 * i, 2)
+        return pltpu.make_async_copy(near_blocks.at[both], near_v.at[both], near_sem.at[i])
 
     def coupling_load(i):
         return pltpu.make_async_copy(leaf_coupling.at[i], coupling_v.at[i], coupling_sem.at[i])
 
-    for load in loads[:3]:
+    for load in loads[:3] + list_loads:
         load.start()
 
     barrier = pltpu.get_barrier_semaphore()
@@ -129,7 +136,7 @@
             barrier, inc=1, device_id=partner, device_id_type=pl.DeviceIdType.MESH
         )
 
-    lax.fori_loop(0, leaves, lambda t, c: (near_load(t).start(), c)[1], 0)
+    lax.fori_loop(0, pairs, lambda i, c: (near_load(i).start(), c)[1], 0)
     for load in loads[3:]:
         load.start()
     lax.fori_loop(0, pairs, lambda i, c: (coupling_load(i).start(), c)[1], 0)
@@ -138,6 +145,15 @@
     leaf_rows[total_leaves] = jnp.zeros((rs, LANES), BF16)
     parent_rows[total_parents] = jnp.zeros((rs, LANES), BF16)
     grand_rows[groups] = jnp.zeros((rs, LANES), BF16)
+
+    for load in list_loads:
+        load.wait()
+    firsts = [me * leaves - reach, 0, 0, 0]
+    zeros = [leaves + 2 * reach, total_leaves, total_parents, groups]
+    for n in range(4):
+        source, valid = lists_v[2 * n][...], lists_v[2 * n + 1][...]
+        places_v[n][...] = jnp.where(valid == 1, source - firsts[n], zeros[n])
+        place_loads[n].start()
 
     pl.semaphore_wait(barrier, len(partners))
 
@@ -219,86 +235,81 @@
         line_copy(i).start()
     spread(0)
 
-    def choose(valid, source, missing):
-        return missing + valid * (source - missing)
-
-    base = me * leaves - reach
-
-    def near_step(t, carry):
-        near_load(t).wait()
-        total = jnp.zeros((rs, width), F32)
+    def near_step(i, carry):
+        near_load(i).wait()
+        sums = [jnp.zeros((rs, width), F32) for h in range(2)]
         for j in range(near_slots):
-            place = choose(near_valid[t, j], near_source[t, j] - base, leaves + 2 * reach)
-            total += dot_nn(slabs[place], near_v[t, j * width : (j + 1) * width, :])
-        near_sum[:, pl.ds(pl.multiple_of(t * width, width), width)] = total
+            for h in range(2):
+                t = 2 * i + h
+                rows = near_v[t, j * width : (j + 1) * width, :]
+                sums[h] += dot_nn(slabs[near_place[j, t]], rows)
+        lanes = pl.ds(pl.multiple_of(2 * i * width, 2 * width), 2 * width)
+        near_sum[:, lanes] = jnp.concatenate(sums, axis=1)
         return carry
 
     for copy in halo:
         copy.wait()
+    for load in place_loads:
+        load.wait()
     for i in range(leaves + 2 * reach):
         slabs[i] = padded[:, i * width : (i + 1) * width]
     cuts = [0]
     for i in range(1, subs):
-        cuts.append(leaves * i // (2 * subs) + 1)
+        cuts.append(pairs * i // (2 * subs) + 1)
         lax.fori_loop(cuts[-2], cuts[-1], near_step, 0)
         spread(i)
     for i in range(subs):
-        cuts.append(leaves if i == subs - 1 else cuts[-1] + (leaves - cuts[-1]) // (subs - i))
+        cuts.append(pairs if i == subs - 1 else cuts[-1] + (pairs - cuts[-1]) // (subs - i))
         lax.fori_loop(cuts[-2], cuts[-1], near_step, 0)
         pass_on(i)
+
+    def duplicate(tile):
+        turned = jnp.concatenate([tile[:, rank:], tile[:, :rank]], axis=1)
+        return jnp.where(low, tile, turned), jnp.where(low, turned, tile)
+
+    def unpack(column, s):
+        d = column * subs + s
+        for i in range(pairs):
+            first, second = duplicate(table[column, s, i])
+            leaf_rows[d * leaves + 2 * i] = first
+            leaf_rows[d * leaves + 2 * i + 1] = second
+        first, second = duplicate(table[column, s, pairs])
+        parent_rows[2 * d] = first
+        parent_rows[2 * d + 1] = second
+
+    for i in range(subs):
+        for k in range(chips):
+            unpack(((chip + chips - k) % chips) * CORES + core, (sub + subs - i) % subs)
     for i in range(subs):
         for k in range(chips):
             twin_copy(i, k).wait_recv()
-
-    def duplicate(tile):
-        turned = jnp.concatenate([tile[:, rank:], tile[:, :rank]], axis=1)
-        return jnp.where(low, tile, turned), jnp.where(low, turned, tile)
-
-    def unpack(d, carry):
-        g, s = d // subs, d % subs
-        for i in range(pairs):
-            first, second = duplicate(table[g, s, i])
-            leaf_rows[d * leaves + 2 * i] = first
-            leaf_rows[d * leaves + 2 * i + 1] = second
-        first, second = duplicate(table[g, s, pairs])
-        parent_rows[2 * d] = first
-        parent_rows[2 * d + 1] = second
-        return carry
-
-    lax.fori_loop(0, total_devices, unpack, 0)
-
-    def gather(rows, source, valid, t, slots, missing):
+            unpack(((chip + chips - k) % chips) * CORES + 1 - core, (sub + subs - i) % subs)
+
+    def gather(rows, place, t, slots):
         parts = []
         for j in range(0, slots, 2):
-            a = rows[choose(valid[t, j], source[t, j], missing)]
-            b = rows[choose(valid[t, j + 1], source[t, j + 1], missing)]
-            parts.append(jnp.where(low, a, b))
+            parts.append(jnp.where(low, rows[place[t, j]], rows[place[t, j + 1]]))
         return jnp.concatenate(parts, axis=1)
 
     for load in loads[3:]:
         load.wait()
-
-    def lift(g, carry):
+    for i in range(pairs):
+        coupling_load(i).wait()
+
+    for g in range(groups):
         up = jnp.concatenate([table[g, s, pairs] for s in range(subs)], axis=1)
         up = dot_nt(up, grand_transfer_v[g]).astype(BF16)
         grand_rows[g] = jnp.concatenate([up, up], axis=1)
-        return carry
-
-    lax.fori_loop(0, groups, lift, 0)
-    picked = gather(grand_rows, grand_source, grand_valid, 0, grand_slots, groups)
+    picked = gather(grand_rows, grand_place, 0, grand_slots)
     grand_total = dot_nt(picked, grand_coupling_v[0]).astype(BF16)
     parent_lanes = pl.ds(pl.multiple_of(sub * LANES, LANES), LANES)
     down_two = dot_nn(grand_total, grand_transfer_v[group, :, parent_lanes])
 
-    def pair_far(rows, source, valid, t, missing, blocks):
-        two = jnp.concatenate(
-            [gather(rows, source, valid, t + h, leaf_slots, missing) for h in range(2)], axis=0
-        )
-        return tile_of(dot_nt(two, blocks))
-
-    parent_far = pair_far(
-        parent_rows, parent_source, parent_valid, 0, total_parents, parent_coupling_v[...]
-    )
+    def pair_far(rows, place, i, blocks):
+        two = [gather(rows, place, 2 * i + h, leaf_slots) for h in range(2)]
+        return tile_of(dot_nt(jnp.concatenate(two, axis=0), blocks))
+
+    parent_far = pair_far(parent_rows, parent_place, 0, parent_coupling_v[...])
     parent_total = (parent_far + down_two).astype(BF16)
     nothing = jnp.zeros((rs, LANES), BF16)
 
@@ -309,22 +320,16 @@
 
     down_one = dot_nn(split(parent_total), transfer_v[...])
     half = pairs // 2
+
     for i in range(pairs):
-        row = (i // half) * rs
-        lane = (i % half) * LANES
-        leaf_far[i] = down_one[row : row + rs, lane : lane + LANES]
-
-    def leaf_step(i, carry):
-        coupling_load(i).wait()
-        far = pair_far(leaf_rows, leaf_source, leaf_valid, 2 * i, total_leaves, coupling_v[i])
-        leaf_total = (far + leaf_far[i]).astype(BF16)
+        row, lane = (i // half) * rs, (i % half) * LANES
+        far = pair_far(leaf_rows, leaf_place, i, coupling_v[i])
+        leaf_total = (far + down_one[row : row + rs, lane : lane + LANES]).astype(BF16)
         both = dot_nn(split(leaf_total), basis_v[i])
         for h in range(2):
-            lanes = pl.ds(pl.multiple_of((2 * i + h) * width, width), width)
-            out[:, lanes] = (both[h * rs : (h + 1) * rs] + near_sum[:, lanes]).astype(BF16)
-        return carry
-
-    lax.fori_loop(0, pairs, leaf_step, 0)
+            start = (2 * i + h) * width
+            summed = both[h * rs : (h + 1) * rs] + near_sum[:, start : start + width]
+            out[:, start : start + width] = summed.astype(BF16)
 
     for i in range(1, subs):
         line_copy(i).wait_send()
@@ -364,13 +369,22 @@
     leaf_coupling = leaf_coupling.reshape(pairs, 2 * rank, leaf_coupling.shape[2])
     parent_transfer = parent_transfer.reshape(2 * rank, parent_transfer.shape[2])
     parent_coupling = parent_coupling.reshape(2 * rank, parent_coupling.shape[2])
-    smem = pl.BlockSpec(memory_space=pltpu.SMEM)
+    lists = [
+        near_source.T,
+        near_valid.T,
+        leaf_source,
+        leaf_valid,
+        parent_source,
+        parent_valid,
+        grand_source,
+        grand_valid,
+    ]
     anywhere = pl.BlockSpec(memory_space=pl.ANY)
     dma = pltpu.SemaphoreType.DMA
     return pl.pallas_call(
         functools.partial(fused_kernel, groups, subs),
         out_shape=jax.ShapeDtypeStruct(densities.shape, BF16),
-        in_specs=[smem] * 8 + [anywhere] * 8,
+        in_specs=[anywhere] * 16,
         out_specs=pl.BlockSpec(memory_space=pltpu.VMEM),
         scratch_shapes=[
             pltpu.VMEM((rs, 2 * leaves * width), BF16),
@@ -387,9 +401,8 @@
             pltpu.VMEM((devices * 2 + 1, rs, LANES), BF16),
             pltpu.VMEM((groups + 1, rs, LANES), BF16),
             pltpu.VMEM((rs, leaves * width), F32),
-            pltpu.VMEM((pairs, rs, LANES), F32),
             dma((6,)),
-            dma((leaves,)),
+            dma((pairs,)),
             dma((pairs,)),
             dma((2,)),
             dma((2,)),
@@ -399,22 +412,20 @@
             dma((subs, chips)),
             dma((subs, chips)),
             dma((subs, chips)),
-        ],
+            dma((8,)),
+            dma((4,)),
+        ]
+        + [pltpu.VMEM(entries.shape, jnp.int32) for entries in lists]
+        + [pltpu.VMEM(entries.shape, jnp.int32) for entries in lists[::2]]
+        + [pltpu.SMEM(entries.shape, jnp.int32) for entries in lists[::2]],
         compiler_params=pltpu.CompilerParams(
-            collective_id=0, has_side_effects=True, vmem_limit_bytes=52 * 1024 * 1024
+            collective_id=0, has_side_effects=True, vmem_limit_bytes=64 * 1024 * 1024
         ),
         cost_estimate=pl.CostEstimate(
             flops=2 * rs * near_blocks.size, bytes_accessed=2 * near_blocks.size, transcendentals=0
         ),
     )(
-        near_source,
-        near_valid,
-        leaf_source,
-        leaf_valid,
-        parent_source,
-        parent_valid,
-        grand_source,
-        grand_valid,
+        *lists,
         densities,
         basis,
         near_blocks,

time: 40.3 us -> 26.1 us (0.65)
  the two profiles are of different devices: /device:TPU:1 before, /device:TPU:0 now
where the time goes in v2:
time: 26.1 us; the launch traced here: 25.9 us
  Pallas kernels  24.3 us (93%)
  local copies, waits for them, and re-layouts  1.57 us (6%)
    pallas_call x1, Pallas kernels, body(): pl.pallas_call(functools.partial(fused_kernel, groups, subs), out_shape=j...  24.3 us
    unnamed x1, local copies, waits for them, and re-layouts  1.57 us

profile of v2, /device:TPU:0, one launch (start us, length us, event | category | flops | bytes accessed | tf_op | source)
XLA Modules:
  0.0 25.9 jit_solution(253849981302262478)
XLA Ops:
  0.0 24.3 %shard_map.154 = bf16[16,4096]{1,0:T(8,128)(2,1)} custom-call(s32[8,16]{1,0:T(8,128)} %bitcast.10, s32[8,16]{1,0:T(8,128)} %bitcast.11, s32[16,32]{1,0:T(8,128)} %refs_2_.1, s32[16,32]{1,0:T(8,128)} %refs_3_.1, s32[2,32]{1,0:T(2,128)} %refs_4_.1, s32[2,32]{1,0:T(2,128)} %refs_5_.1, s32[1,16]{1,0:T(1,128)} %refs_6_.1, s32[1,16]{1,0:T(1,128)} %refs_7_.1, ...), custom_call_target="tpu_custom_call" | custom-call | flops 268435456 | bytes 16777216 | tf_op jit(solution)/shard_map/pallas_call | solution.py:384
  24.3 1.6 %copy.18 = bf16[16,4096]{1,0:T(8,128)(2,1)} copy(bf16[16,4096]{1,0:T(8,128)(2,1)} %shard_map.154) | data formatting | bytes 262144

commit v3 on v2

--- a/solution.py
+++ b/solution.py
@@ -21,39 +21,30 @@
     return lax.dot_general(a, b, (((1,), (0,)), ((), ())), preferred_element_type=F32)
 
 
-def fused_kernel(
+def near_kernel(
     groups,
     subs,
-    *refs,
-):
-    lists, refs = refs[:8], refs[8:]
-    (
+    near_source,
+    near_valid,
     densities,
     basis,
     near_blocks,
-    leaf_coupling,
     parent_transfer,
-    parent_coupling,
-    grand_transfer,
-    grand_coupling,
-    out,
+    out_table,
+    out_near,
     padded,
     slabs,
     basis_v,
     near_v,
-    coupling_v,
     transfer_v,
-    parent_coupling_v,
-    grand_transfer_v,
-    grand_coupling_v,
     table,
-    leaf_rows,
-    parent_rows,
-    grand_rows,
     near_sum,
+    source_v,
+    valid_v,
+    place_v,
+    near_place,
     load_sem,
     near_sem,
-    coupling_sem,
     halo_send,
     halo_recv,
     line_send,
@@ -62,22 +53,15 @@
     plane_recv,
     twin_send,
     twin_recv,
-    list_sem,
-    place_sem,
-    ), refs = refs[:36], refs[36:]
-    lists_v, places_v, places = refs[:8], refs[8:12], refs[12:]
-    near_place, leaf_place, parent_place, grand_place = places
+    keep_sem,
+):
     rs = densities.shape[0]
     pairs, pair_rank, width = basis.shape
     leaves = 2 * pairs
     rank = pair_rank // 2
     reach = leaves // 2
-    near_slots = lists[0].shape[0]
-    leaf_slots = lists[2].shape[1]
-    grand_slots = lists[6].shape[1]
+    near_slots = near_source.shape[0]
     total_devices = groups * subs
-    total_leaves = total_devices * leaves
-    total_parents = total_devices * 2
     chips = groups // CORES
     low = lax.broadcasted_iota(jnp.int32, (rs, LANES), 1) < rank
 
@@ -106,26 +90,16 @@
         ),
         pltpu.make_async_copy(basis, basis_v, load_sem.at[1]),
         pltpu.make_async_copy(parent_transfer, transfer_v, load_sem.at[2]),
-        pltpu.make_async_copy(grand_transfer, grand_transfer_v, load_sem.at[3]),
-        pltpu.make_async_copy(parent_coupling, parent_coupling_v, load_sem.at[4]),
-        pltpu.make_async_copy(grand_coupling, grand_coupling_v, load_sem.at[5]),
+        pltpu.make_async_copy(near_source, source_v, load_sem.at[3]),
+        pltpu.make_async_copy(near_valid, valid_v, load_sem.at[4]),
     ]
-
-    list_loads = [
-        pltpu.make_async_copy(lists[n], lists_v[n], list_sem.at[n]) for n in range(8)
-    ]
-    place_loads = [
-        pltpu.make_async_copy(places_v[n], places[n], place_sem.at[n]) for n in range(4)
-    ]
+    place_load = pltpu.make_async_copy(place_v, near_place, load_sem.at[5])
 
     def near_load(i):
         both = pl.ds(2 * i, 2)
         return pltpu.make_async_copy(near_blocks.at[both], near_v.at[both], near_sem.at[i])
 
-    def coupling_load(i):
-        return pltpu.make_async_copy(leaf_coupling.at[i], coupling_v.at[i], coupling_sem.at[i])
-
-    for load in loads[:3] + list_loads:
+    for load in loads:
         load.start()
 
     barrier = pltpu.get_barrier_semaphore()
@@ -137,23 +111,13 @@
         )
 
     lax.fori_loop(0, pairs, lambda i, c: (near_load(i).start(), c)[1], 0)
+    slabs[leaves + 2 * reach] = jnp.zeros((rs, width), BF16)
+
     for load in loads[3:]:
-        load.start()
-    lax.fori_loop(0, pairs, lambda i, c: (coupling_load(i).start(), c)[1], 0)
-
-    slabs[leaves + 2 * reach] = jnp.zeros((rs, width), BF16)
-    leaf_rows[total_leaves] = jnp.zeros((rs, LANES), BF16)
-    parent_rows[total_parents] = jnp.zeros((rs, LANES), BF16)
-    grand_rows[groups] = jnp.zeros((rs, LANES), BF16)
-
-    for load in list_loads:
         load.wait()
-    firsts = [me * leaves - reach, 0, 0, 0]
-    zeros = [leaves + 2 * reach, total_leaves, total_parents, groups]
-    for n in range(4):
-        source, valid = lists_v[2 * n][...], lists_v[2 * n + 1][...]
-        places_v[n][...] = jnp.where(valid == 1, source - firsts[n], zeros[n])
-        place_loads[n].start()
+    local = source_v[...] - (me * leaves - reach)
+    place_v[...] = jnp.where(valid_v[...] == 1, local, leaves + 2 * reach)
+    place_load.start()
 
     pl.semaphore_wait(barrier, len(partners))
 
@@ -249,8 +213,7 @@
 
     for copy in halo:
         copy.wait()
-    for load in place_loads:
-        load.wait()
+    place_load.wait()
     for i in range(leaves + 2 * reach):
         slabs[i] = padded[:, i * width : (i + 1) * width]
     cuts = [0]
@@ -263,6 +226,117 @@
         lax.fori_loop(cuts[-2], cuts[-1], near_step, 0)
         pass_on(i)
 
+    def keep(i, k, other):
+        column = ((chip + chips - k) % chips) * CORES + (1 - core if other else core)
+        block = (column, (sub + subs - i) % subs)
+        n = 2 * (i * chips + k) + int(other)
+        return pltpu.make_async_copy(table.at[block], out_table.at[block], keep_sem.at[n])
+
+    sums_out = pltpu.make_async_copy(near_sum, out_near, load_sem.at[3])
+    sums_out.start()
+    blocks = [(i, k) for i in range(subs) for k in range(chips)]
+    for i, k in blocks:
+        keep(i, k, False).start()
+    for i, k in blocks:
+        twin_copy(i, k).wait_recv()
+        keep(i, k, True).start()
+    for i, k in blocks:
+        keep(i, k, False).wait()
+        keep(i, k, True).wait()
+    sums_out.wait()
+
+    for i in range(1, subs):
+        line_copy(i).wait_send()
+    for i in range(subs):
+        for k in range(chips):
+            if k > 0:
+                plane_copy(i, k).wait_send()
+            twin_copy(i, k).wait_send()
+
+
+def far_kernel(groups, subs, *refs):
+    lists, refs = refs[:6], refs[6:]
+    (
+        table_h,
+        near_h,
+        basis,
+        leaf_coupling,
+        parent_transfer,
+        parent_coupling,
+        grand_transfer,
+        grand_coupling,
+        out,
+        table,
+        near_sum,
+        basis_v,
+        coupling_v,
+        transfer_v,
+        parent_coupling_v,
+        grand_transfer_v,
+        grand_coupling_v,
+        leaf_rows,
+        parent_rows,
+        grand_rows,
+        load_sem,
+        table_sem,
+        coupling_sem,
+        list_sem,
+        place_sem,
+    ) = refs[:25]
+    lists_v, places_v, places = refs[25:31], refs[31:34], refs[34:]
+    leaf_place, parent_place, grand_place = places
+    pairs, pair_rank, width = basis.shape
+    rs = near_h.shape[0]
+    leaves = 2 * pairs
+    rank = pair_rank // 2
+    leaf_slots = lists[0].shape[1]
+    grand_slots = lists[4].shape[1]
+    total_leaves = groups * subs * leaves
+    total_parents = groups * subs * 2
+    low = lax.broadcasted_iota(jnp.int32, (rs, LANES), 1) < rank
+    group = lax.axis_index("leaf")
+    sub = lax.axis_index("sub")
+
+    def tile_of(both):
+        return jnp.where(low, both[:rs], both[rs:])
+
+    held = [
+        (grand_transfer, grand_transfer_v),
+        (grand_coupling, grand_coupling_v),
+        (parent_coupling, parent_coupling_v),
+        (parent_transfer, transfer_v),
+        (basis, basis_v),
+        (near_h, near_sum),
+    ]
+    loads = [pltpu.make_async_copy(a, b, load_sem.at[n]) for n, (a, b) in enumerate(held)]
+    list_loads = [
+        pltpu.make_async_copy(lists[n], lists_v[n], list_sem.at[n]) for n in range(6)
+    ]
+    place_loads = [
+        pltpu.make_async_copy(places_v[n], places[n], place_sem.at[n]) for n in range(3)
+    ]
+
+    def table_load(column):
+        return pltpu.make_async_copy(table_h.at[column], table.at[column], table_sem.at[column])
+
+    def coupling_load(i):
+        return pltpu.make_async_copy(leaf_coupling.at[i], coupling_v.at[i], coupling_sem.at[i])
+
+    for load in list_loads + [table_load(column) for column in range(groups)] + loads:
+        load.start()
+    for i in range(pairs):
+        coupling_load(i).start()
+    leaf_rows[total_leaves] = jnp.zeros((rs, LANES), BF16)
+    parent_rows[total_parents] = jnp.zeros((rs, LANES), BF16)
+    grand_rows[groups] = jnp.zeros((rs, LANES), BF16)
+
+    for load in list_loads:
+        load.wait()
+    zeros = [total_leaves, total_parents, groups]
+    for n in range(3):
+        places_v[n][...] = jnp.where(lists_v[2 * n + 1][...] == 1, lists_v[2 * n][...], zeros[n])
+        place_loads[n].start()
+
     def duplicate(tile):
         turned = jnp.concatenate([tile[:, rank:], tile[:, :rank]], axis=1)
         return jnp.where(low, tile, turned), jnp.where(low, turned, tile)
@@ -277,13 +351,12 @@
         parent_rows[2 * d] = first
         parent_rows[2 * d + 1] = second
 
-    for i in range(subs):
-        for k in range(chips):
-            unpack(((chip + chips - k) % chips) * CORES + core, (sub + subs - i) % subs)
-    for i in range(subs):
-        for k in range(chips):
-            twin_copy(i, k).wait_recv()
-            unpack(((chip + chips - k) % chips) * CORES + 1 - core, (sub + subs - i) % subs)
+    for column in range(groups):
+        table_load(column).wait()
+        for s in range(subs):
+            unpack(column, s)
+    for load in place_loads:
+        load.wait()
 
     def gather(rows, place, t, slots):
         parts = []
@@ -291,7 +364,7 @@
             parts.append(jnp.where(low, rows[place[t, j]], rows[place[t, j + 1]]))
         return jnp.concatenate(parts, axis=1)
 
-    for load in loads[3:]:
+    for load in loads:
         load.wait()
     for i in range(pairs):
         coupling_load(i).wait()
@@ -330,14 +403,6 @@
             start = (2 * i + h) * width
             summed = both[h * rs : (h + 1) * rs] + near_sum[:, start : start + width]
             out[:, start : start + width] = summed.astype(BF16)
-
-    for i in range(1, subs):
-        line_copy(i).wait_send()
-    for i in range(subs):
-        for k in range(chips):
-            if k > 0:
-                plane_copy(i, k).wait_send()
-            twin_copy(i, k).wait_send()
 
 
 def body(
@@ -369,40 +434,30 @@
     leaf_coupling = leaf_coupling.reshape(pairs, 2 * rank, leaf_coupling.shape[2])
     parent_transfer = parent_transfer.reshape(2 * rank, parent_transfer.shape[2])
     parent_coupling = parent_coupling.reshape(2 * rank, parent_coupling.shape[2])
-    lists = [
-        near_source.T,
-        near_valid.T,
-        leaf_source,
-        leaf_valid,
-        parent_source,
-        parent_valid,
-        grand_source,
-        grand_valid,
-    ]
     anywhere = pl.BlockSpec(memory_space=pl.ANY)
     dma = pltpu.SemaphoreType.DMA
-    return pl.pallas_call(
-        functools.partial(fused_kernel, groups, subs),
-        out_shape=jax.ShapeDtypeStruct(densities.shape, BF16),
-        in_specs=[anywhere] * 16,
-        out_specs=pl.BlockSpec(memory_space=pltpu.VMEM),
+    near_lists = near_source.T.shape
+    table = (groups, subs, pairs + 1, rs, LANES)
+    sums = (rs, leaves * width)
+    limit = 64 * 1024 * 1024
+    every, near = pl.pallas_call(
+        functools.partial(near_kernel, groups, subs),
+        out_shape=[jax.ShapeDtypeStruct(table, BF16), jax.ShapeDtypeStruct(sums, F32)],
+        in_specs=[anywhere] * 6,
+        out_specs=[anywhere] * 2,
         scratch_shapes=[
             pltpu.VMEM((rs, 2 * leaves * width), BF16),
             pltpu.VMEM((2 * leaves + 1, rs, width), BF16),
             pltpu.VMEM(basis.shape, BF16),
             pltpu.VMEM(near_blocks.shape, BF16),
-            pltpu.VMEM(leaf_coupling.shape, BF16),
             pltpu.VMEM(parent_transfer.shape, BF16),
-            pltpu.VMEM(parent_coupling.shape, BF16),
-            pltpu.VMEM(grand_transfer.shape, BF16),
-            pltpu.VMEM(grand_coupling.shape, BF16),
-            pltpu.VMEM((groups, subs, pairs + 1, rs, LANES), BF16),
-            pltpu.VMEM((devices * leaves + 1, rs, LANES), BF16),
-            pltpu.VMEM((devices * 2 + 1, rs, LANES), BF16),
-            pltpu.VMEM((groups + 1, rs, LANES), BF16),
-            pltpu.VMEM((rs, leaves * width), F32),
+            pltpu.VMEM(table, BF16),
+            pltpu.VMEM(sums, F32),
+            pltpu.VMEM(near_lists, jnp.int32),
+            pltpu.VMEM(near_lists, jnp.int32),
+            pltpu.VMEM(near_lists, jnp.int32),
+            pltpu.SMEM(near_lists, jnp.int32),
             dma((6,)),
-            dma((pairs,)),
             dma((pairs,)),
             dma((2,)),
             dma((2,)),
@@ -412,23 +467,51 @@
             dma((subs, chips)),
             dma((subs, chips)),
             dma((subs, chips)),
-            dma((8,)),
-            dma((4,)),
+            dma((2 * subs * chips,)),
+        ],
+        compiler_params=pltpu.CompilerParams(
+            collective_id=0, has_side_effects=True, vmem_limit_bytes=limit
+        ),
+        cost_estimate=pl.CostEstimate(
+            flops=2 * rs * near_blocks.size, bytes_accessed=2 * near_blocks.size, transcendentals=0
+        ),
+    )(near_source.T, near_valid.T, densities, basis, near_blocks, parent_transfer)
+    lists = [leaf_source, leaf_valid, parent_source, parent_valid, grand_source, grand_valid]
+    return pl.pallas_call(
+        functools.partial(far_kernel, groups, subs),
+        out_shape=jax.ShapeDtypeStruct(densities.shape, BF16),
+        in_specs=[anywhere] * 14,
+        out_specs=pl.BlockSpec(memory_space=pltpu.VMEM),
+        scratch_shapes=[
+            pltpu.VMEM(table, BF16),
+            pltpu.VMEM(sums, F32),
+            pltpu.VMEM(basis.shape, BF16),
+            pltpu.VMEM(leaf_coupling.shape, BF16),
+            pltpu.VMEM(parent_transfer.shape, BF16),
+            pltpu.VMEM(parent_coupling.shape, BF16),
+            pltpu.VMEM(grand_transfer.shape, BF16),
+            pltpu.VMEM(grand_coupling.shape, BF16),
+            pltpu.VMEM((devices * leaves + 1, rs, LANES), BF16),
+            pltpu.VMEM((devices * 2 + 1, rs, LANES), BF16),
+            pltpu.VMEM((groups + 1, rs, LANES), BF16),
+            dma((6,)),
+            dma((groups,)),
+            dma((pairs,)),
+            dma((6,)),
+            dma((3,)),
         ]
         + [pltpu.VMEM(entries.shape, jnp.int32) for entries in lists]
         + [pltpu.VMEM(entries.shape, jnp.int32) for entries in lists[::2]]
         + [pltpu.SMEM(entries.shape, jnp.int32) for entries in lists[::2]],
-        compiler_params=pltpu.CompilerParams(
-            collective_id=0, has_side_effects=True, vmem_limit_bytes=64 * 1024 * 1024
-        ),
+        compiler_params=pltpu.CompilerParams(vmem_limit_bytes=limit),
         cost_estimate=pl.CostEstimate(
-            flops=2 * rs * near_blocks.size, bytes_accessed=2 * near_blocks.size, transcendentals=0
+            flops=2 * rs * leaf_coupling.size, bytes_accessed=2 * leaf_coupling.size, transcendentals=0
         ),
     )(
         *lists,
-        densities,
+        every,
+        near,
         basis,
-        near_blocks,
         leaf_coupling,
         parent_transfer,
         parent_coupling,

time: 26.1 us -> 28.9 us (1.11)
  the two profiles are of different devices: /device:TPU:0 before, /device:TPU:1 now
where the time goes in v3:
time: 28.9 us; the launch traced here: 28.8 us
  Pallas kernels  28.8 us (100%)
    pallas_call x1, Pallas kernels, body(): pl.pallas_call(functools.partial(near_kernel, groups, subs), out_shape=[j...  20.1 us
    pallas_call x1, Pallas kernels, body(): pl.pallas_call(functools.partial(far_kernel, groups, subs), out_shape=jax...  8.68 us

profile of v3, /device:TPU:1, one launch (start us, length us, event | category | flops | bytes accessed | tf_op | source)
XLA Modules:
  0.0 28.8 jit_solution(15823292552129645141)
XLA Ops:
  0.0 20.1 %shard_map.154 = (bf16[8,4,9,16,128]{4,3,2,1,0:T(8,128)(2,1)}, f32[16,4096]{1,0:T(8,128)}) custom-call(s32[8,16]{1,0:T(8,128)} %bitcast.12, s32[8,16]{1,0:T(8,128)} %bitcast.13, bf16[16,4096]{1,0:T(8,128)(2,1)} %densities.1, bf16[8,128,256]{2,1,0:T(8,128)(2,1)} %bitcast.7, bf16[16,2048,256]{2,1,0:T(8,128)(2,1)} %near_blocks.1, bf16[128,512]{1,0:T(8,128)(2,1)} %bitcast.9), custom_call_target="tpu_custom_call" | custom-call | flops 268435456 | bytes 16777216 | tf_op jit(solution)/shard_map/pallas_call | solution.py:443
  20.1 8.7 %shard_map.155 = bf16[16,4096]{1,0:T(8,128)(2,1)} custom-call(s32[16,32]{1,0:T(8,128)} %refs_0_.1, s32[16,32]{1,0:T(8,128)} %refs_1_.1, s32[2,32]{1,0:T(2,128)} %refs_2_.1, s32[2,32]{1,0:T(2,128)} %refs_3_.1, s32[1,16]{1,0:T(1,128)} %refs_4_.1, s32[1,16]{1,0:T(1,128)} %refs_5_.1, bf16[8,4,9,16,128]{4,3,2,1,0:T(8,128)(2,1)} %get-tuple-element.7.refs_6_, ...), custom_call_target="tpu_custom_call" | custom-call | flops 67108864 | bytes 4194304 | tf_op jit(solution)/shard_map/pallas_call | solution.py:480

commit v4 on v2

--- a/solution.py
+++ b/solution.py
@@ -146,15 +146,6 @@
     parent_rows[total_parents] = jnp.zeros((rs, LANES), BF16)
     grand_rows[groups] = jnp.zeros((rs, LANES), BF16)
 
-    for load in list_loads:
-        load.wait()
-    firsts = [me * leaves - reach, 0, 0, 0]
-    zeros = [leaves + 2 * reach, total_leaves, total_parents, groups]
-    for n in range(4):
-        source, valid = lists_v[2 * n][...], lists_v[2 * n + 1][...]
-        places_v[n][...] = jnp.where(valid == 1, source - firsts[n], zeros[n])
-        place_loads[n].start()
-
     pl.semaphore_wait(barrier, len(partners))
 
     def remote(src, dst, send, recv, device):
@@ -169,24 +160,25 @@
 
     halo = [
         remote(
-            densities.at[:, own_width - reach_width :],
+            padded.at[:, own_width : reach_width + own_width],
             padded.at[:, :reach_width],
             halo_send.at[0],
             halo_recv.at[0],
             following,
         ),
         remote(
-            densities.at[:, :reach_width],
+            padded.at[:, reach_width : 2 * reach_width],
             padded.at[:, reach_width + own_width :],
             halo_send.at[1],
             halo_recv.at[1],
             previous,
         ),
     ]
+    loads[0].wait()
     for copy in halo:
         copy.start()
 
-    for load in loads[:3]:
+    for load in loads[1:3]:
         load.wait()
 
     def tile_of(both):
@@ -235,17 +227,41 @@
         line_copy(i).start()
     spread(0)
 
-    def near_step(i, carry):
+    for load in list_loads:
+        load.wait()
+    firsts = [me * leaves - reach, 0, 0, 0]
+    zeros = [leaves + 2 * reach, total_leaves, total_parents, groups]
+    for n in range(4):
+        source, valid = lists_v[2 * n][...], lists_v[2 * n + 1][...]
+        places_v[n][...] = jnp.where(valid == 1, source - firsts[n], zeros[n])
+        place_loads[n].start()
+
+    def duplicate(tile):
+        turned = jnp.concatenate([tile[:, rank:], tile[:, :rank]], axis=1)
+        return jnp.where(low, tile, turned), jnp.where(low, turned, tile)
+
+    def unpack(i, k, other):
+        column = ((chip + chips - k) % chips) * CORES + (1 - core if other else core)
+        s = (sub + subs - i) % subs
+        d = column * subs + s
+        for n in range(pairs):
+            first, second = duplicate(table[column, s, n])
+            leaf_rows[d * leaves + 2 * n] = first
+            leaf_rows[d * leaves + 2 * n + 1] = second
+        first, second = duplicate(table[column, s, pairs])
+        parent_rows[2 * d] = first
+        parent_rows[2 * d + 1] = second
+
+    def near_step(i):
         near_load(i).wait()
-        sums = [jnp.zeros((rs, width), F32) for h in range(2)]
-        for j in range(near_slots):
-            for h in range(2):
-                t = 2 * i + h
-                rows = near_v[t, j * width : (j + 1) * width, :]
-                sums[h] += dot_nn(slabs[near_place[j, t]], rows)
-        lanes = pl.ds(pl.multiple_of(2 * i * width, 2 * width), 2 * width)
-        near_sum[:, lanes] = jnp.concatenate(sums, axis=1)
-        return carry
+        for t in (2 * i, 2 * i + 1):
+            picked = [slabs[near_place[j, t]] for j in range(near_slots)]
+            total = dot_nn(jnp.concatenate(picked, axis=1), near_v[t])
+            near_sum[:, t * width : (t + 1) * width] = total
+
+    def twin_wait(i):
+        for k in range(chips):
+            twin_copy(i, k).wait_recv()
 
     for copy in halo:
         copy.wait()
@@ -253,37 +269,31 @@
         load.wait()
     for i in range(leaves + 2 * reach):
         slabs[i] = padded[:, i * width : (i + 1) * width]
-    cuts = [0]
-    for i in range(1, subs):
-        cuts.append(pairs * i // (2 * subs) + 1)
-        lax.fori_loop(cuts[-2], cuts[-1], near_step, 0)
-        spread(i)
-    for i in range(subs):
-        cuts.append(pairs if i == subs - 1 else cuts[-1] + (pairs - cuts[-1]) // (subs - i))
-        lax.fori_loop(cuts[-2], cuts[-1], near_step, 0)
-        pass_on(i)
-
-    def duplicate(tile):
-        turned = jnp.concatenate([tile[:, rank:], tile[:, :rank]], axis=1)
-        return jnp.where(low, tile, turned), jnp.where(low, turned, tile)
-
-    def unpack(column, s):
-        d = column * subs + s
-        for i in range(pairs):
-            first, second = duplicate(table[column, s, i])
-            leaf_rows[d * leaves + 2 * i] = first
-            leaf_rows[d * leaves + 2 * i + 1] = second
-        first, second = duplicate(table[column, s, pairs])
-        parent_rows[2 * d] = first
-        parent_rows[2 * d + 1] = second
-
-    for i in range(subs):
+    actions = [(1, i) for i in range(1, subs)] + [(2, i) for i in range(subs)]
+    for n in range(max(pairs, len(actions))):
+        if n < pairs:
+            near_step(n)
+        if n < len(actions):
+            kind, i = actions[n]
+            if kind == 1:
+                spread(i)
+                unpack(i - 1, 0, False)
+            else:
+                pass_on(i)
+                if i == 0:
+                    unpack(subs - 1, 0, False)
+                if i >= 2:
+                    twin_wait(i - 2)
+                for k in range(chips):
+                    if k > 0:
+                        unpack(i, k, False)
+                    if i >= 2:
+                        unpack(i - 2, k, True)
+    for i in range(max(subs - 2, 0), subs):
+        twin_wait(i)
+    for i in range(max(subs - 2, 0), subs):
         for k in range(chips):
-            unpack(((chip + chips - k) % chips) * CORES + core, (sub + subs - i) % subs)
-    for i in range(subs):
-        for k in range(chips):
-            twin_copy(i, k).wait_recv()
-            unpack(((chip + chips - k) % chips) * CORES + 1 - core, (sub + subs - i) % subs)
+            unpack(i, k, True)
 
     def gather(rows, place, t, slots):
         parts = []
@@ -329,7 +339,7 @@
         for h in range(2):
             start = (2 * i + h) * width
             summed = both[h * rs : (h + 1) * rs] + near_sum[:, start : start + width]
-            out[:, start : start + width] = summed.astype(BF16)
+            out[:, start : start + width] = summed
 
     for i in range(1, subs):
         line_copy(i).wait_send()
@@ -383,7 +393,7 @@
     dma = pltpu.SemaphoreType.DMA
     return pl.pallas_call(
         functools.partial(fused_kernel, groups, subs),
-        out_shape=jax.ShapeDtypeStruct(densities.shape, BF16),
+        out_shape=jax.ShapeDtypeStruct(densities.shape, F32),
         in_specs=[anywhere] * 16,
         out_specs=pl.BlockSpec(memory_space=pltpu.VMEM),
         scratch_shapes=[
@@ -434,7 +444,7 @@
         parent_coupling,
         grand_transfer,
         grand_coupling,
-    )
+    ).astype(BF16)
 
 
 def solution(mesh):

time: 26.1 us -> 24.4 us (0.935)
  the two profiles are of different devices: /device:TPU:0 before, /device:TPU:1 now
where the time goes in v4:
time: 24.4 us; the launch traced here: 24.2 us
  Pallas kernels  22.6 us (93%)
  other arithmetic  1.62 us (7%)
    pallas_call x1, Pallas kernels, body(): pl.pallas_call(functools.partial(fused_kernel, groups, subs), out_shape=j...  22.6 us
    convert_element_type x1, other arithmetic, body(): return pl.pallas_call(functools.partial(fused_kernel, groups, subs), out_...  1.62 us

profile of v4, /device:TPU:1, one launch (start us, length us, event | category | flops | bytes accessed | tf_op | source)
XLA Modules:
  0.0 24.2 jit_solution(846031473294021779)
XLA Ops:
  0.0 22.6 %shard_map.154 = f32[16,4096]{1,0:T(8,128)} custom-call(s32[8,16]{1,0:T(8,128)} %bitcast.10, s32[8,16]{1,0:T(8,128)} %bitcast.11, s32[16,32]{1,0:T(8,128)} %refs_2_.1, s32[16,32]{1,0:T(8,128)} %refs_3_.1, s32[2,32]{1,0:T(2,128)} %refs_4_.1, s32[2,32]{1,0:T(2,128)} %refs_5_.1, s32[1,16]{1,0:T(1,128)} %refs_6_.1, s32[1,16]{1,0:T(1,128)} %refs_7_.1, ...), custom_call_target="tpu_custom_call" | custom-call | flops 268435456 | bytes 16777216 | tf_op jit(solution)/shard_map/pallas_call | solution.py:394
  22.6 1.6 %convert_element_type.3 = bf16[16,4096]{1,0:T(8,128)(2,1)} convert(f32[16,4096]{1,0:T(8,128)} %shard_map.154) | non-fusion elementwise | flops 65536 | bytes 393216 | tf_op jit(solution)/shard_map/convert_element_type | solution.py:447

commit v5 on v4

--- a/solution.py
+++ b/solution.py
@@ -289,6 +289,10 @@
                         unpack(i, k, False)
                     if i >= 2:
                         unpack(i - 2, k, True)
+    for load in loads[3:]:
+        load.wait()
+    for i in range(pairs):
+        coupling_load(i).wait()
     for i in range(max(subs - 2, 0), subs):
         twin_wait(i)
     for i in range(max(subs - 2, 0), subs):
@@ -300,11 +304,6 @@
         for j in range(0, slots, 2):
             parts.append(jnp.where(low, rows[place[t, j]], rows[place[t, j + 1]]))
         return jnp.concatenate(parts, axis=1)
-
-    for load in loads[3:]:
-        load.wait()
-    for i in range(pairs):
-        coupling_load(i).wait()
 
     for g in range(groups):
         up = jnp.concatenate([table[g, s, pairs] for s in range(subs)], axis=1)
@@ -339,7 +338,7 @@
         for h in range(2):
             start = (2 * i + h) * width
             summed = both[h * rs : (h + 1) * rs] + near_sum[:, start : start + width]
-            out[:, start : start + width] = summed
+            out[:, start : start + width] = summed.astype(BF16)
 
     for i in range(1, subs):
         line_copy(i).wait_send()
@@ -393,7 +392,7 @@
     dma = pltpu.SemaphoreType.DMA
     return pl.pallas_call(
         functools.partial(fused_kernel, groups, subs),
-        out_shape=jax.ShapeDtypeStruct(densities.shape, F32),
+        out_shape=jax.ShapeDtypeStruct(densities.shape, BF16),
         in_specs=[anywhere] * 16,
         out_specs=pl.BlockSpec(memory_space=pltpu.VMEM),
         scratch_shapes=[
@@ -444,7 +443,7 @@
         parent_coupling,
         grand_transfer,
         grand_coupling,
-    ).astype(BF16)
+    )
 
 
 def solution(mesh):

time: 24.4 us -> 24.1 us (0.988)
  other arithmetic: 1.62 us -> 0 us
  local copies, waits for them, and re-layouts: 0 us -> 1.57 us
    convert_element_type x1 -> x0, other arithmetic: 1.62 us -> none  [body(): return pl.pallas_call(functools.partial(fused_kernel, groups, subs), out_...]
    unnamed x0 -> x1, local copies, waits for them, and re-layouts: none -> 1.57 us
where the time goes in v5:
time: 24.1 us; the launch traced here: 24 us
  Pallas kernels  22.4 us (93%)
  local copies, waits for them, and re-layouts  1.57 us (7%)
    pallas_call x1, Pallas kernels, body(): pl.pallas_call(functools.partial(fused_kernel, groups, subs), out_shape=j...  22.4 us
    unnamed x1, local copies, waits for them, and re-layouts  1.57 us

profile of v5, /device:TPU:1, one launch (start us, length us, event | category | flops | bytes accessed | tf_op | source)
XLA Modules:
  0.0 24.0 jit_solution(5502057624626139700)
XLA Ops:
  0.0 22.4 %shard_map.154 = bf16[16,4096]{1,0:T(8,128)(2,1)} custom-call(s32[8,16]{1,0:T(8,128)} %bitcast.10, s32[8,16]{1,0:T(8,128)} %bitcast.11, s32[16,32]{1,0:T(8,128)} %refs_2_.1, s32[16,32]{1,0:T(8,128)} %refs_3_.1, s32[2,32]{1,0:T(2,128)} %refs_4_.1, s32[2,32]{1,0:T(2,128)} %refs_5_.1, s32[1,16]{1,0:T(1,128)} %refs_6_.1, s32[1,16]{1,0:T(1,128)} %refs_7_.1, ...), custom_call_target="tpu_custom_call" | custom-call | flops 268435456 | bytes 16777216 | tf_op jit(solution)/shard_map/pallas_call | solution.py:393
  22.4 1.6 %copy.18 = bf16[16,4096]{1,0:T(8,128)(2,1)} copy(bf16[16,4096]{1,0:T(8,128)(2,1)} %shard_map.154) | data formatting | bytes 262144
